TPU v7x, 256 devices: a whole 4x4x8 slice. The times are simulated.
256 devices in a mesh: ctx: 8 (over y, core), br: 32 (over z, x).
Axes of the slice: x: 4, y: 4, z: 8, core: 2. Of those that a mesh axis runs over, the one named last changes fastest.
Arguments:
- prompt_key_value: bfloat16 [2, 16384, 1024], P(None, 'ctx'), may hold values from -10 to 10
- suffix_page_store: bfloat16 [1024, 2, 128, 1024], P('br', None, None, 'ctx'), may hold values from -8 to 8
- page_table: int32 [512, 2], P('br'), may hold values from 0 to 1023, as said below
- lengths: int32 [512], replicated, may hold values from 1 to 253
- parents: int32 [3, 512], replicated, may hold values from 0 to 511, as said below
- queries: bfloat16 [3, 512, 8192], P(None, 'br', 'ctx'), may hold values from -6.4 to 6.4
- fresh_key_value: bfloat16 [3, 2, 512, 1024], P(None, None, 'br', 'ctx'), may hold values from -8 to 8
Outputs:
- attention: bfloat16 [3, 512, 8192], P(None, 'br', 'ctx')
Inputs may be any that keep to these rules, and one draw needn't show every extreme that they name: `page_table`: the 2 pages of the 16 branches of one device of br are exactly that device's 16 * 2 pages of suffix_page_store, each named once. The branches of one device of br form aligned groups of 1 consecutive branches; all parents of one group lie on one device of br, and different groups of one device take their parents from different devices.
All inputs are finite; a program needn't handle non-finite values.
Results may differ from a plain program's by a relative error of at most 0.002.
Values may be sent and summed in bfloat16 or wider, within the bound.
A program may use at most 128 MiB of HBM per device.

v0:
```python
import math

import jax
import jax.numpy as jnp
from jax import lax
from jax.sharding import PartitionSpec as P

QUERY_HEADS = 64
KEY_VALUE_HEADS = 8
HEAD_SIZE = 128


NEG_FILL = -1e30


def joined_2(part, axis, combine):
    gathered = jax.tree.map(lambda a: lax.all_gather(a, axis), part)

    def take(source):
        return jax.tree.map(lambda a: lax.dynamic_index_in_dim(a, source, 0, False), gathered)

    return lax.fori_loop(
        1, lax.axis_size(axis), lambda source, state: combine(state, take(source)), take(0)
    )


def block_stats(scores, values, einsum_form):
    peak_value = jnp.max(scores, axis=-1)
    weights = jnp.exp(scores - peak_value[..., None])
    weight_total = jnp.sum(weights, axis=-1)
    rounded = weights.astype(jnp.bfloat16)
    summed = jnp.einsum(einsum_form, rounded, values, preferred_element_type=jnp.float32)
    return (peak_value, weight_total, summed)


def fold_pair(left_stats, right_stats):
    peak_value = jnp.maximum(left_stats[0], right_stats[0])
    left_weight = jnp.exp(left_stats[0] - peak_value)
    right_weight = jnp.exp(right_stats[0] - peak_value)
    weight_total = left_stats[1] * left_weight + right_stats[1] * right_weight
    summed = left_stats[2] * left_weight[..., None] + right_stats[2] * right_weight[..., None]
    return (peak_value, weight_total, summed)


def suffix_stats(query_head_rows, suffix_tokens, live_length, score_scale):
    row_count = suffix_tokens.shape[0]
    suffix_length = suffix_tokens.shape[2]
    kv_local = query_head_rows.shape[1]
    branch_suffix_keys = suffix_tokens[:, 0].reshape(row_count, suffix_length, kv_local, HEAD_SIZE)
    branch_suffix_values = suffix_tokens[:, 1].reshape(
        row_count, suffix_length, kv_local, HEAD_SIZE
    )
    scores = (
        jnp.einsum(
            "bgrd,btgd->bgrt",
            query_head_rows,
            branch_suffix_keys,
            preferred_element_type=jnp.float32,
        )
        * score_scale
    )
    live_mask = jnp.arange(suffix_length, dtype=jnp.int32)[None, :] < live_length[:, None]
    scores = jnp.where(live_mask[:, None, None, :], scores, NEG_FILL)
    return block_stats(scores, branch_suffix_values, "bgrt,btgd->bgrd")


def routing(parent, branch_per_shard, br_index, slot_rank, slot_match):
    grid_owner = (parent // branch_per_shard).reshape(-1, branch_per_shard)
    grid_local = (parent % branch_per_shard).reshape(-1, branch_per_shard)
    matched = (grid_owner == br_index)[:, :, None] & slot_match[None, :, :]
    outgoing = jnp.sum(jnp.where(matched, grid_local[:, :, None], 0), axis=1)
    own_owner = (
        lax.dynamic_slice_in_dim(parent, br_index * branch_per_shard, branch_per_shard)
        // branch_per_shard
    )
    incoming = own_owner * slot_match.shape[1] + slot_rank
    return (outgoing, incoming, own_owner)


def move_suffix(suffix_tokens, outgoing, incoming):
    dest_count = outgoing.shape[0]
    slot_count = outgoing.shape[1]
    tail_shape = suffix_tokens.shape[1:]
    outbound = suffix_tokens[outgoing.reshape(-1)].reshape((dest_count, slot_count) + tail_shape)
    arrived = lax.all_to_all(outbound, "br", split_axis=0, concat_axis=0, tiled=True)
    return arrived.reshape((dest_count * slot_count,) + tail_shape)[incoming]


def append_token(suffix_tokens, position_at, fresh_token):
    suffix_length = suffix_tokens.shape[2]
    target_mask = jnp.arange(suffix_length, dtype=jnp.int32)[None, :] == position_at[:, None]
    return jnp.where(
        target_mask[:, None, :, None], jnp.swapaxes(fresh_token, 0, 1)[:, :, None, :], suffix_tokens
    )


def local(
    prompt_key_value, suffix_page_store, page_table, lengths, parents, queries, fresh_key_value
):
    br_count = lax.axis_size("br")
    br_index = lax.axis_index("br")
    ctx_index = lax.axis_index("ctx")
    branch_per_shard = page_table.shape[0]
    page_count = page_table.shape[1]
    pool_dev = suffix_page_store.shape[0]
    page_rows = suffix_page_store.shape[2]
    head_width = suffix_page_store.shape[3]
    step_count = queries.shape[0]
    kv_local = head_width // HEAD_SIZE
    group_width = QUERY_HEADS // KEY_VALUE_HEADS
    slot_count = max(1, branch_per_shard // br_count)
    score_scale = 1.0 / math.sqrt(HEAD_SIZE)
    slot_rank = jnp.arange(branch_per_shard, dtype=jnp.int32) % slot_count
    slot_match = slot_rank[:, None] == jnp.arange(slot_count, dtype=jnp.int32)[None, :]
    gathered_pages = suffix_page_store[page_table - br_index * pool_dev]
    suffix_tokens = jnp.swapaxes(gathered_pages, 1, 2).reshape(
        branch_per_shard, 2, page_count * page_rows, head_width
    )
    length = lengths
    head_listing = lax.all_gather(queries, "ctx", axis=2, tiled=True)
    shared_prompt_keys = prompt_key_value[0].reshape(-1, KEY_VALUE_HEADS, HEAD_SIZE)
    shared_prompt_values = prompt_key_value[1].reshape(-1, KEY_VALUE_HEADS, HEAD_SIZE)
    outputs = []
    for decode_step_index in range(step_count):
        parent = parents[decode_step_index]
        outgoing, incoming, own_owner = routing(
            parent, branch_per_shard, br_index, slot_rank, slot_match
        )
        parent_length = length[parent]
        own_parent_length = lax.dynamic_slice_in_dim(
            parent_length, br_index * branch_per_shard, branch_per_shard
        )
        fresh_token = fresh_key_value[decode_step_index]
        query_mine = queries[decode_step_index].reshape(
            branch_per_shard, kv_local, group_width, HEAD_SIZE
        )
        suffix_tokens = append_token(
            move_suffix(suffix_tokens, outgoing, incoming), own_parent_length, fresh_token
        )
        suffix_part = suffix_stats(query_mine, suffix_tokens, own_parent_length + 1, score_scale)
        length = parent_length + 1
        query_complete = head_listing[decode_step_index].reshape(
            branch_per_shard, KEY_VALUE_HEADS, group_width, HEAD_SIZE
        )
        prompt_scores = (
            jnp.einsum(
                "bgrd,tgd->bgrt",
                query_complete,
                shared_prompt_keys,
                preferred_element_type=jnp.float32,
            )
            * score_scale
        )
        prompt_part = block_stats(prompt_scores, shared_prompt_values, "bgrt,tgd->bgrd")
        head_start = ctx_index * kv_local
        own_heads = tuple(
            (lax.dynamic_slice_in_dim(member, head_start, kv_local, 1) for member in prompt_part)
        )
        joined = fold_pair(own_heads, suffix_part)
        placed = tuple(
            (
                lax.dynamic_update_slice_in_dim(whole_part, own_part, head_start, 1)
                for whole_part, own_part in zip(prompt_part, joined)
            )
        )
        merged = joined_2((placed[0], placed[1], placed[2]), "ctx", fold_pair)
        combined = tuple(
            (lax.dynamic_slice_in_dim(member, head_start, kv_local, 1) for member in merged)
        )
        attention = (combined[2] / combined[1][..., None]).reshape(
            branch_per_shard, kv_local * group_width * HEAD_SIZE
        )
        outputs.append(attention.astype(jnp.bfloat16))
    return jnp.stack(outputs)


def solution(mesh):
    in_specs = (
        P(None, "ctx", None),
        P("br", None, None, "ctx"),
        P("br", None),
        P(),
        P(),
        P(None, "br", "ctx"),
        P(None, None, "br", "ctx"),
    )
    out_specs = P(None, "br", "ctx")
    return jax.shard_map(local, mesh=mesh, in_specs=in_specs, out_specs=out_specs, check_vma=False)
```

profile of v0, /device:TPU:6, one launch (start us, length us, event | category | flops | bytes accessed | tf_op | source)
XLA Modules:
  0.0 464.6 jit_solution(1010023589338554495)
XLA Ops:
  7.6 2.0 slice_reduce_fusion
  9.9 2.2 gather_fusion.1
  12.1 1.7 copy.165
  13.8 3.1 gather_fusion.2
  16.9 11.8 %all-to-all-start = ((bf16[32,1,2,256,128]{4,3,2,1,0:T(8,128)(2,1)}), bf16[32,1,2,256,128]{4,3,2,1,0:T(8,128)(2,1)}, u32[]{:S(2)}, u32[]{:S(2)}) async-start(bf16[32,1,2,256,128]{4,3,2,1,0:T(8,128)(2,1)} %bitcast.418), calls=%async_computation | async-start | bytes 8388608 | tf_op jit(solution)/shard_map/all_to_all | solution.py:85
  29.3 3.5 gather_fusion
  33.7 13.9 %all_gather.75 = bf16[3,16,8192]{2,1,0:T(8,128)(2,1)S(1)} all-gather(bf16[3,16,1024]{2,1,0:T(8,128)(2,1)S(1)} %copy-done.15), channel_id=1, replica_groups=mesh['ctx'=8,'br'=32] {'ctx'}, dimensions={2}, use_global_device_ids=true | all-gather | bytes 884736 | tf_op jit(solution)/shard_map/all_gather | solution.py:120
  47.6 76.9 %all-to-all-done = bf16[32,1,2,256,128]{4,3,2,1,0:T(8,128)(2,1)} async-done(((bf16[32,1,2,256,128]{4,3,2,1,0:T(8,128)(2,1)}), bf16[32,1,2,256,128]{4,3,2,1,0:T(8,128)(2,1)}, u32[]{:S(2)}, u32[]{:S(2)}) %all-to-all-start) | async-done | bytes 4194336 | tf_op jit(solution)/shard_map/all_to_all | solution.py:85
  124.4 4.4 gather_fusion.3
  128.8 2.8 copy_select_fusion.2
  131.6 3.1 gather_fusion.5
  134.7 5.5 %all-to-all-start.1 = ((bf16[32,1,2,256,128]{4,3,2,1,0:T(8,128)(2,1)}), bf16[32,1,2,256,128]{4,3,2,1,0:T(8,128)(2,1)}, u32[]{:S(2)}, u32[]{:S(2)}) async-start(bf16[32,1,2,256,128]{4,3,2,1,0:T(8,128)(2,1)} %bitcast.416), calls=%async_computation.1 | async-start | bytes 8388608 | tf_op jit(solution)/shard_map/all_to_all | solution.py:85
  142.3 5.9 %fusion.111 = (bf16[1,2048,1024]{2,1,0:T(8,128)(2,1)}, bf16[1,2048,1024]{2,1,0:T(8,128)(2,1)}) fusion(bf16[2,2048,1024]{2,1,0:T(8,128)(2,1)} %param.13), kind=kLoop, calls=%fused_computation.273 | loop fusion | bytes 16777216 | tf_op jit(solution)/shard_map/slice | solution.py:122
  148.2 6.5 %copy.214 = bf16[1,2048,1024]{1,2,0:T(8,128)(2,1)} copy(bf16[1,2048,1024]{2,1,0:T(8,128)(2,1)} %get-tuple-element.668) | data formatting | bytes 8388608
  154.7 6.5 %copy.213 = bf16[1,2048,1024]{1,2,0:T(8,128)(2,1)} copy(bf16[1,2048,1024]{2,1,0:T(8,128)(2,1)} %get-tuple-element.669) | data formatting | bytes 8388608
  161.3 3.8 bitcast_reduce_fusion.2
  165.1 1.9 fusion.22
  175.0 3.5 gather_fusion.4
  179.1 3.5 gather_fusion.7
  184.2 51.9 %all-to-all-done.1 = bf16[32,1,2,256,128]{4,3,2,1,0:T(8,128)(2,1)} async-done(((bf16[32,1,2,256,128]{4,3,2,1,0:T(8,128)(2,1)}), bf16[32,1,2,256,128]{4,3,2,1,0:T(8,128)(2,1)}, u32[]{:S(2)}, u32[]{:S(2)}) %all-to-all-start.1) | async-done | bytes 4194336 | tf_op jit(solution)/shard_map/all_to_all | solution.py:85
  236.1 4.3 gather_fusion.6
  240.4 2.8 copy_select_fusion.1
  243.2 3.0 gather_fusion.8
  246.3 5.6 %all-to-all-start.2 = ((bf16[32,1,2,256,128]{4,3,2,1,0:T(8,128)(2,1)}), bf16[32,1,2,256,128]{4,3,2,1,0:T(8,128)(2,1)}, u32[]{:S(2)}, u32[]{:S(2)}) async-start(bf16[32,1,2,256,128]{4,3,2,1,0:T(8,128)(2,1)} %bitcast.417), calls=%async_computation.2 | async-start | bytes 8388608 | tf_op jit(solution)/shard_map/all_to_all | solution.py:85
  252.2 3.8 bitcast_reduce_fusion.1
  256.0 1.9 fusion.20
  264.1 3.8 bitcast_reduce_fusion
  268.0 1.6 fusion.17
  270.2 2.0 copy-done.8
  273.2 6.6 %fusion.18 = f32[8,16,8,128]{3,1,2,0:T(8,128)S(1)} fusion(bf16[2048,8,128,1]{0,2,3,1:T(8,128)(2,1)S(1)} %bitcast.410, f32[8,2048,16,8]{1,2,3,0:T(8,128)} %copy-done.8, f32[16,8,8]{0,2,1:T(8,128)S(1)} %get-tuple-element.697), kind=kOutput, calls=%fused_computation.49 | convolution fusion | flops 543162368 | bytes 13111296 | tf_op jit(solution)/shard_map/bgrt,tgd->bgrd/dot_general | solution.py:32
  280.6 1.6 fusion.15
  283.6 1.6 fusion.13
  288.2 13.7 %all_gather.81 = f32[8,16,8,8]{1,3,2,0:T(8,128)S(1)} all-gather(f32[1,16,8,8]{1,3,2,0:T(8,128)S(1)} %get-tuple-element.678), channel_id=1, replica_groups=mesh['ctx'=8,'br'=32] {'ctx'}, dimensions={0}, use_global_device_ids=true | all-gather | bytes 36864 | tf_op jit(solution)/shard_map/all_gather | solution.py:17
  301.9 13.0 %all_gather.78 = f32[8,16,8,8]{1,3,2,0:T(8,128)S(1)} all-gather(f32[1,16,8,8]{1,3,2,0:T(8,128)S(1)} %get-tuple-element.679), channel_id=1, replica_groups=mesh['ctx'=8,'br'=32] {'ctx'}, dimensions={0}, use_global_device_ids=true | all-gather | bytes 36864 | tf_op jit(solution)/shard_map/all_gather | solution.py:17
  316.7 31.0 %all-to-all-done.2 = bf16[32,1,2,256,128]{4,3,2,1,0:T(8,128)(2,1)} async-done(((bf16[32,1,2,256,128]{4,3,2,1,0:T(8,128)(2,1)}), bf16[32,1,2,256,128]{4,3,2,1,0:T(8,128)(2,1)}, u32[]{:S(2)}, u32[]{:S(2)}) %all-to-all-start.2) | async-done | bytes 4194336 | tf_op jit(solution)/shard_map/all_to_all | solution.py:85
  347.8 3.3 gather_fusion.9
  355.0 1.5 fusion.36
  357.3 2.0 copy.193
  359.4 17.2 %while.57 = (s32[]{:T(128)}, f32[16,8,8]{0,2,1:T(8,128)S(1)}, f32[16,8,8]{0,2,1:T(8,128)S(1)}, f32[16,8,8,128]{3,2,1,0:T(8,128)S(1)}, f32[8,16,8,8]{1,3,2,0:T(8,...) while((s32[]{:T(128)}, f32[16,8,8]{0,2,1:T(8,128)S(1)}, ...), condition=%wide.region_6.7_spmd, body=%wide.region_5.6_spmd.sunk | while | flops 399365 | bytes 1630351 | solution.py:22
  360.4 1.4 fusion.131
  362.9 1.4 fusion.131
  365.3 1.4 fusion.131
  367.8 1.5 fusion.131
  370.3 1.4 fusion.131
  372.7 1.4 fusion.131
  375.2 1.4 fusion.131
  377.8 13.7 %all_gather.90 = f32[8,16,8,8]{1,3,2,0:T(8,128)S(1)} all-gather(f32[1,16,8,8]{1,3,2,0:T(8,128)S(1)} %get-tuple-element.682), channel_id=1, replica_groups=mesh['ctx'=8,'br'=32] {'ctx'}, dimensions={0}, use_global_device_ids=true | all-gather | bytes 36864 | tf_op jit(solution)/shard_map/all_gather | solution.py:17
  391.5 12.8 %all_gather.87 = f32[8,16,8,8]{1,3,2,0:T(8,128)S(1)} all-gather(f32[1,16,8,8]{1,3,2,0:T(8,128)S(1)} %get-tuple-element.683), channel_id=1, replica_groups=mesh['ctx'=8,'br'=32] {'ctx'}, dimensions={0}, use_global_device_ids=true | all-gather | bytes 36864 | tf_op jit(solution)/shard_map/all_gather | solution.py:17
  405.5 11.8 %while.58 = (s32[]{:T(128)}, f32[16,8,8]{0,2,1:T(8,128)S(1)}, f32[16,8,8]{0,2,1:T(8,128)S(1)}, f32[16,8,8,128]{3,2,1,0:T(8,128)S(1)}, f32[8,16,8,8]{1,3,2,0:T(8,...) while((s32[]{:T(128)}, f32[16,8,8]{0,2,1:T(8,128)S(1)}, ...), condition=%wide.region_13.14_spmd, body=%wide.region_12.13_spmd.sunk | while | flops 399365 | bytes 1630351 | solution.py:22
  405.7 1.4 fusion.133
  407.4 1.4 fusion.133
  409.1 1.4 fusion.133
  410.8 1.4 fusion.133
  412.5 1.4 fusion.133
  414.2 1.4 fusion.133
  415.9 1.4 fusion.133
  418.5 12.8 %all_gather.99 = f32[8,16,8,8]{1,3,2,0:T(8,128)S(1)} all-gather(f32[1,16,8,8]{1,3,2,0:T(8,128)S(1)} %get-tuple-element.686), channel_id=1, replica_groups=mesh['ctx'=8,'br'=32] {'ctx'}, dimensions={0}, use_global_device_ids=true | all-gather | bytes 36864 | tf_op jit(solution)/shard_map/all_gather | solution.py:17
  431.3 12.8 %all_gather.96 = f32[8,16,8,8]{1,3,2,0:T(8,128)S(1)} all-gather(f32[1,16,8,8]{1,3,2,0:T(8,128)S(1)} %get-tuple-element.687), channel_id=1, replica_groups=mesh['ctx'=8,'br'=32] {'ctx'}, dimensions={0}, use_global_device_ids=true | all-gather | bytes 36864 | tf_op jit(solution)/shard_map/all_gather | solution.py:17
  445.2 11.9 %while.59 = (s32[]{:T(128)}, f32[16,8,8]{0,2,1:T(8,128)S(1)}, f32[16,8,8]{0,2,1:T(8,128)S(1)}, f32[16,8,8,128]{3,2,1,0:T(8,128)S(1)}, f32[8,16,8,8]{1,3,2,0:T(8,...) while((s32[]{:T(128)}, f32[16,8,8]{0,2,1:T(8,128)S(1)}, ...), condition=%wide.region_20.21_spmd, body=%wide.region_19.20_spmd.sunk | while | flops 399365 | bytes 1630351 | solution.py:22
  445.5 1.6 fusion.135
  447.3 1.4 fusion.135
  449.0 1.4 fusion.135
  450.7 1.4 fusion.135
  452.4 1.4 fusion.135
  (264 shorter events, 52.5 us)
Async XLA Ops:
  6.5 3.4 copy-start
  16.9 11.8 %copy-start.33 = (s32[3,512]{1,0:T(4,128)S(1)}, s32[3,512]{1,0:T(4,128)}, u32[]{:S(2)}) copy-start(s32[3,512]{1,0:T(4,128)} %param.17) | copy-start | bytes 18436
  16.9 12.4 %copy-start.2 = (s32[512]{0:T(512)S(1)}, s32[512]{0:T(512)}, u32[]{:S(2)}) copy-start(s32[512]{0:T(512)} %param.16) | copy-start | bytes 6148
  16.9 16.2 %copy-start.32 = (bf16[3,2,16,128]{3,2,1,0:T(8,128)(2,1)S(1)}, bf16[3,2,16,128]{3,2,1,0:T(8,128)(2,1)}, u32[]{:S(2)}) copy-start(bf16[3,2,16,128]{3,2,1,0:T(8,128)(2,1)} %param.19) | copy-start | bytes 73732
  16.9 16.8 %copy-start.15 = (bf16[3,16,1024]{2,1,0:T(8,128)(2,1)S(1)}, bf16[3,16,1024]{2,1,0:T(8,128)(2,1)}, u32[]{:S(2)}) copy-start(bf16[3,16,1024]{2,1,0:T(8,128)(2,1)} %param.18) | copy-start | bytes 294916
  16.9 107.5 %all-to-all-start = ((bf16[32,1,2,256,128]{4,3,2,1,0:T(8,128)(2,1)}), bf16[32,1,2,256,128]{4,3,2,1,0:T(8,128)(2,1)}, u32[]{:S(2)}, u32[]{:S(2)}) async-start(bf16[32,1,2,256,128]{4,3,2,1,0:T(8,128)(2,1)} %bitcast.418), calls=%async_computation | async-start | bytes 8388608 | tf_op jit(solution)/shard_map/all_to_all | solution.py:85
  32.8 96.0 %copy-start.35 = (s32[512]{0:T(512)}, s32[512]{0:T(512)S(1)}, u32[]{:S(2)}) copy-start(s32[512]{0:T(512)S(1)} %gather_fusion) | copy-start | bytes 6148
  134.7 101.4 %all-to-all-start.1 = ((bf16[32,1,2,256,128]{4,3,2,1,0:T(8,128)(2,1)}), bf16[32,1,2,256,128]{4,3,2,1,0:T(8,128)(2,1)}, u32[]{:S(2)}, u32[]{:S(2)}) async-start(bf16[32,1,2,256,128]{4,3,2,1,0:T(8,128)(2,1)} %bitcast.416), calls=%async_computation.1 | async-start | bytes 8388608 | tf_op jit(solution)/shard_map/all_to_all | solution.py:85
  140.2 175.5 %all-gather.4.cloned.1.call-start = ((), (), s32[]{:S(2)}) async-start(), calls=%async_computation.3 | async-start | bytes 4718592 | tf_op jit(solution)/shard_map/all_gather | solution.py:17
  161.3 3.8 copy-start.3
  165.1 3.3 copy-start.6
  165.1 3.3 copy-start.19
  169.7 70.8 %copy-start.13 = (f32[16,8,256]{2,1,0:T(8,128)}, f32[16,8,256]{2,1,0:T(8,128)S(1)}, u32[]{:S(2)}) copy-start(f32[16,8,256]{2,1,0:T(8,128)S(1)} %get-tuple-element.708) | copy-start | bytes 393220
  169.7 70.7 %copy-start.28 = (f32[16,8]{0,1:T(8,128)}, f32[16,8]{0,1:T(8,128)S(1)}, u32[]{:S(2)}) copy-start(f32[16,8]{0,1:T(8,128)S(1)} %copy.168) | copy-start | bytes 1540
  175.0 65.5 %copy-start.30 = (bf16[16,2,128]{2,0,1:T(8,128)(2,1)S(1)}, bf16[16,2,128]{2,0,1:T(8,128)(2,1)}, u32[]{:S(2)}) copy-start(bf16[16,2,128]{2,0,1:T(8,128)(2,1)} %get-tuple-element.690) | copy-start | bytes 24580
  246.3 101.5 %all-to-all-start.2 = ((bf16[32,1,2,256,128]{4,3,2,1,0:T(8,128)(2,1)}), bf16[32,1,2,256,128]{4,3,2,1,0:T(8,128)(2,1)}, u32[]{:S(2)}, u32[]{:S(2)}) async-start(bf16[32,1,2,256,128]{4,3,2,1,0:T(8,128)(2,1)} %bitcast.417), calls=%async_computation.2 | async-start | bytes 8388608 | tf_op jit(solution)/shard_map/all_to_all | solution.py:85
  251.9 152.4 %all-gather.6.cloned.1.call-start = ((), (), s32[]{:S(2)}) async-start(), calls=%async_computation.4 | async-start | bytes 4718592 | tf_op jit(solution)/shard_map/all_gather | solution.py:17
  252.2 3.8 copy-start.26
  252.2 3.8 copy-start.4
  256.0 3.3 copy-start.7
  256.0 3.3 copy-start.17
  256.0 3.3 copy-start.39
  259.8 8.1 %copy-start.11 = (f32[16,8,256]{2,1,0:T(8,128)}, f32[16,8,256]{2,1,0:T(8,128)S(1)}, u32[]{:S(2)}) copy-start(f32[16,8,256]{2,1,0:T(8,128)S(1)} %get-tuple-element.704) | copy-start | bytes 393220
  262.6 181.5 %all-gather.8.cloned.1.call-start = ((), (), s32[]{:S(2)}) async-start(), calls=%async_computation.5 | async-start | bytes 4718592 | tf_op jit(solution)/shard_map/all_gather | solution.py:17
  264.1 16.5 %slice-start.2 = ((s8[8388608]{0:T(1024)(128)(4,1)}), s8[4194304]{0:T(1024)(128)(4,1)S(1)}, s32[]{:S(2)}) async-start(s8[8388608]{0:T(1024)(128)(4,1)} %bitcast.413), calls=%async_computation.8 | async-start | bytes 8388608
  267.9 4.3 copy-start.8
  267.9 4.9 %copy-start.16 = (f32[16,8,8]{0,2,1:T(8,128)}, f32[16,8,8]{0,2,1:T(8,128)S(1)}, u32[]{:S(2)}) copy-start(f32[16,8,8]{0,2,1:T(8,128)S(1)} %get-tuple-element.697) | copy-start | bytes 12292
  267.9 5.3 %copy-start.5 = (bf16[1,2048,1024]{1,2,0:T(8,128)(2,1)S(1)}, bf16[1,2048,1024]{1,2,0:T(8,128)(2,1)}, u32[]{:S(2)}) copy-start(bf16[1,2048,1024]{1,2,0:T(8,128)(2,1)} %copy.214) | copy-start | bytes 12582916
  267.9 12.7 %slice-start.3 = ((s8[8388608]{0:T(1024)(128)(4,1)}), s8[4194304]{0:T(1024)(128)(4,1)S(1)}, s32[]{:S(2)}) async-start(s8[8388608]{0:T(1024)(128)(4,1)} %bitcast.413), calls=%async_computation.9 | async-start | bytes 8388608
  272.2 11.3 %slice-start = ((s8[8388608]{0:T(1024)(128)(4,1)}), s8[4194304]{0:T(1024)(128)(4,1)S(1)}, s32[]{:S(2)}) async-start(s8[8388608]{0:T(1024)(128)(4,1)} %bitcast.411), calls=%async_computation.6 | async-start | bytes 8388608
  273.2 7.4 %copy-start.18 = (f32[16,8,8]{0,2,1:T(8,128)S(1)}, f32[16,8,8]{0,2,1:T(8,128)}, u32[]{:S(2)}) copy-start(f32[16,8,8]{0,2,1:T(8,128)} %copy-done.17) | copy-start | bytes 12292
  273.2 10.4 %slice-start.1 = ((s8[8388608]{0:T(1024)(128)(4,1)}), s8[4194304]{0:T(1024)(128)(4,1)S(1)}, s32[]{:S(2)}) async-start(s8[8388608]{0:T(1024)(128)(4,1)} %bitcast.411), calls=%async_computation.7 | async-start | bytes 8388608
  280.6 2.9 copy-start.20
  282.3 3.0 copy-start.21
  283.6 3.0 copy-start.38
  283.6 3.6 copy-start.37
  283.6 4.3 copy-start.14
  283.6 4.6 copy-start.29
  288.1 63.0 %copy-start.34 = (pred[16,256]{1,0:T(8,128)(4,1)S(1)}, pred[16,256]{1,0:T(8,128)(4,1)}, u32[]{:S(2)}) copy-start(pred[16,256]{1,0:T(8,128)(4,1)} %iota_compare_fusion) | copy-start | bytes 12292
  314.9 0.7 copy-start.10
  347.7 6.0 %copy-start.36 = (pred[16,256]{1,0:T(8,128)(4,1)S(1)}, pred[16,256]{1,0:T(8,128)(4,1)}, u32[]{:S(2)}) copy-start(pred[16,256]{1,0:T(8,128)(4,1)} %iota_compare_fusion.1) | copy-start | bytes 12292
  351.0 2.8 copy-start.31
  352.5 1.3 copy-start.9
  359.3 17.5 %copy-start.12 = (f32[16,8,256]{2,1,0:T(8,128)S(1)}, f32[16,8,256]{2,1,0:T(8,128)}, u32[]{:S(2)}) copy-start(f32[16,8,256]{2,1,0:T(8,128)} %copy-done.11) | copy-start | bytes 393220
  359.4 17.7 %copy-start.24 = (f32[1,16,8,8]{1,3,2,0:T(8,128)S(1)}, f32[1,16,8,8]{1,3,2,0:T(8,128)}, u32[]{:S(2)}) copy-start(f32[1,16,8,8]{1,3,2,0:T(8,128)} %copy.272) | copy-start | bytes 12292
  359.4 17.7 %copy-start.25 = (f32[1,16,8,8]{1,3,2,0:T(8,128)S(1)}, f32[1,16,8,8]{1,3,2,0:T(8,128)}, u32[]{:S(2)}) copy-start(f32[1,16,8,8]{1,3,2,0:T(8,128)} %copy.273) | copy-start | bytes 12292
  359.4 17.7 %copy-start.27 = (f32[16,8]{0,1:T(8,128)S(1)}, f32[16,8]{0,1:T(8,128)}, u32[]{:S(2)}) copy-start(f32[16,8]{0,1:T(8,128)} %copy.179) | copy-start | bytes 1540
  405.5 12.3 %copy-start.22 = (f32[1,16,8,8]{1,3,2,0:T(8,128)S(1)}, f32[1,16,8,8]{1,3,2,0:T(8,128)}, u32[]{:S(2)}) copy-start(f32[1,16,8,8]{1,3,2,0:T(8,128)} %copy.257) | copy-start | bytes 12292
  405.5 12.3 %copy-start.23 = (f32[1,16,8,8]{1,3,2,0:T(8,128)S(1)}, f32[1,16,8,8]{1,3,2,0:T(8,128)}, u32[]{:S(2)}) copy-start(f32[1,16,8,8]{1,3,2,0:T(8,128)} %copy.258) | copy-start | bytes 12292
  445.2 12.8 %copy-start.1 = (bf16[32,2,128,128]{3,2,1,0:T(8,128)(2,1)S(1)}, bf16[32,2,128,128]{3,2,1,0:T(8,128)(2,1)}, u32[]{:S(2)}) copy-start(bf16[32,2,128,128]{3,2,1,0:T(8,128)(2,1)} %param.14) | copy-start | bytes 6291460
Sparse Core Ops, SparseCore 0:
  172.0 35.8 all-gather.3
  262.7 36.2 all-gather.5
  359.5 32.3 all-gather.7
where the time goes:
time: 469 us; the launch traced here: 465 us
  waiting for transfers between devices  160 us (34%)
  blocking collectives  92.9 us (20%)
  local copies, waits for them, and re-layouts  85.4 us (18%)
  other arithmetic  62.6 us (13%)
  matrix products  26 us (6%)
  starting transfers between devices  23.2 us (5%)
  between operations  13.8 us (3%)
    all_to_all x3, waiting for transfers between devices, move_suffix(): lax.all_to_all(outbound, 'br', split_axis=0, concat_axis=0, tiled=True)  160 us
    all_gather x6, blocking collectives, joined_2(): gathered = jax.tree.map(lambda a: lax.all_gather(a, axis), part)  79 us
    add x21, other arithmetic, fold_pair(): left_stats[2] * left_weight[..., None]  30.4 us
    unnamed x107, local copies, waits for them, and re-layouts  28.1 us
    all_to_all x3, starting transfers between devices, move_suffix(): lax.all_to_all(outbound, 'br', split_axis=0, concat_axis=0, tiled=True)  22.9 us
    all_gather x1, blocking collectives, local(): head_listing = lax.all_gather(queries, 'ctx', axis=2, tiled=True)  13.9 us
    dot_general x6, matrix products, block_stats(): jnp.einsum(einsum_form, rounded, values, preferred_element_type=jnp.float32)  12.5 us
    gather x3, local copies, waits for them, and re-layouts, move_suffix(): return arrived.reshape((dest_count * slot_count,) + tail_shape)[incoming]  12 us
  transfers between devices with their start and end apart: 6, of which 3 were waited for; matrix products, arithmetic and copies ran while one was open for 29% of the time, Pallas kernels for 0%

commit v1 on v0

--- a/solution.py
+++ b/solution.py
@@ -1,8 +1,11 @@
+import functools
 import math
 
 import jax
 import jax.numpy as jnp
 from jax import lax
+from jax.experimental import pallas as pl
+from jax.experimental.pallas import tpu as pltpu
 from jax.sharding import PartitionSpec as P
 
 QUERY_HEADS = 64
@@ -94,7 +97,7 @@
     )
 
 
-def local(
+def general(
     prompt_key_value, suffix_page_store, page_table, lengths, parents, queries, fresh_key_value
 ):
     br_count = lax.axis_size("br")
@@ -174,6 +177,428 @@
     return jnp.stack(outputs)
 
 
+STEPS = 3
+BRANCHES = 16
+NODES = STEPS * BRANCHES
+CAP = 8
+LIVE = 96
+FIRST = 16
+KEYS = 4096
+ROWS = 8 * NODES
+MASKED = -1e30
+EXP_SCALE = math.log2(math.e) / math.sqrt(HEAD_SIZE)
+BF = jnp.bfloat16
+F32 = jnp.float32
+NT = (((1,), (1,)), ((), ()))
+
+
+def onehot(condition):
+    return jnp.where(condition, 1.0, 0.0).astype(BF)
+
+
+def iota(shape, axis):
+    return lax.broadcasted_iota(jnp.int32, shape, axis)
+
+
+def stacked(rows, count, width):
+    at = iota((count, width), 0)
+    out = jnp.zeros((count, width), F32)
+    for index, row in enumerate(rows):
+        out = jnp.where(at == index, row.astype(F32), out)
+    return out.astype(BF)
+
+
+def dot(left, right):
+    return jnp.dot(left, right, preferred_element_type=F32)
+
+
+def dot_nt(left, right):
+    return lax.dot_general(left, right, NT, preferred_element_type=F32)
+
+
+def softmax_block(query, key, value):
+    raw = dot_nt(query, key)
+    peak = jnp.max(raw, axis=1, keepdims=True)
+    weight = jnp.exp2((raw - peak) * EXP_SCALE)
+    total = jnp.sum(weight, axis=1, keepdims=True)
+    return peak, total, dot(weight.astype(BF), value)
+
+
+def kernel(
+    br_count, ctx_count,
+    page_ref, len_ref, par_ref, q_ref, fresh_ref, pkv_ref, pages_ref,
+    out_ref, flag_ref,
+    kbuf, vbuf, kcat, vcat, qbuf, sendm, recvm, qcat, part_send, part_recv, suffix_out, ret_send, ret_recv, num,
+    kv_sem, page_sem, q_send, q_recv, m_send, m_recv, p_send, p_recv, r_send, r_recv,
+):
+    me_c = lax.axis_index("ctx")
+    me_r = lax.axis_index("br")
+
+    def peer_c(i):
+        return lax.rem(me_c + i, ctx_count)
+
+    def peer_r(i):
+        return lax.rem(me_r + i, br_count)
+
+    def head_at(i):
+        chip = lax.rem(me_c // 2 + i // 2, ctx_count // 2)
+        return chip * 2 + lax.rem(me_c + lax.rem(i, 2), 2)
+
+    barrier = pltpu.get_barrier_semaphore()
+
+    @pl.loop(1, ctx_count)
+    def _(i):
+        pl.semaphore_signal(barrier, inc=1, device_id={"ctx": peer_c(i)}, device_id_type=pl.DeviceIdType.MESH)
+
+    @pl.loop(1, br_count)
+    def _(i):
+        pl.semaphore_signal(barrier, inc=1, device_id={"br": peer_r(i)}, device_id_type=pl.DeviceIdType.MESH)
+
+    def kv_copy(i, which):
+        g = head_at(i)
+        buffer = kbuf if which == 0 else vbuf
+        return pltpu.make_async_copy(
+            pkv_ref.at[which, :, pl.ds(pl.multiple_of(g * HEAD_SIZE, HEAD_SIZE), HEAD_SIZE)],
+            buffer.at[g], kv_sem.at[which, g])
+
+    key_pages = pltpu.make_async_copy(pages_ref.at[:, 0], kcat.at[pl.ds(0, 32), :, pl.ds(0, HEAD_SIZE)], page_sem.at[0])
+    value_pages = pltpu.make_async_copy(pages_ref.at[:, 1], vcat.at[pl.ds(0, 32)], page_sem.at[1])
+
+    @pl.loop(0, ctx_count)
+    def _(i):
+        kv_copy(i, 0).start()
+        kv_copy(i, 1).start()
+
+    key_pages.start()
+    value_pages.start()
+
+    parent = par_ref[...]
+    device = lax.shift_right_logical(parent, 4)
+    place = parent & 15
+    width = parent.shape[1]
+    row_at = iota((width, width), 0)
+    pick1 = onehot(row_at == parent[1:2])
+    pick2 = onehot(row_at == parent[2:3])
+    first = dot(stacked([device[0:1], place[0:1]], 16, width), pick1)
+    second = dot(stacked([first[0:1], first[1:2], device[1:2], place[1:2]], 16, width), pick2)
+    anc_dev = [device[0:1].astype(F32), first[0:1], second[0:1]]
+    anc_loc = [place[0:1].astype(F32), first[1:2], second[1:2]]
+    missing = jnp.full((1, width), -1.0, F32)
+    par_hi = [missing, device[1:2].astype(F32), device[2:3].astype(F32) + 32.0]
+    par_lo = [missing, place[1:2].astype(F32), place[2:3].astype(F32)]
+    old_hi = [missing, missing, second[2:3]]
+    old_lo = [missing, missing, second[3:4]]
+
+    owner = iota((br_count, width), 0).astype(F32)
+    to_owner = [onehot(owner == anc_dev[s]) for s in range(STEPS)]
+    j = iota((128, 256), 0)
+    lane = iota((128, 256), 1)
+    b = lane & 127
+    same_home = (j >> 4) == (b >> 4)
+    counting = onehot(same_home & ((lane >= 128) | (j < b)))
+    slots = [[], [], []]
+    pair_count = []
+    for tile in range(width // 128):
+        cut = [m[:, tile * 128:(tile + 1) * 128] for m in to_owner]
+        counted = dot(jnp.concatenate(cut, axis=0), counting)
+        before = jnp.zeros((br_count, 128), F32)
+        for s in range(STEPS):
+            block = counted[s * br_count:(s + 1) * br_count]
+            slots[s].append(jnp.sum(cut[s].astype(F32) * (block[:, :128] + before), axis=0, keepdims=True))
+            before = before + block[:, 128:]
+        pair_count.append(before)
+    slot = [jnp.concatenate(parts, axis=1) for parts in slots]
+    count = jnp.concatenate(pair_count, axis=1)
+    most = jnp.max(count)
+    fullest = jnp.max(jnp.sum(count, axis=1, keepdims=True)) / BRANCHES
+    over = (most > CAP) | (fullest > LIVE)
+    flag_ref[...] = jnp.where(over, 1, 0) + jnp.zeros((8, 128), jnp.int32)
+
+    node = iota((128, STEPS * width), 0)
+    column = iota((128, STEPS * width), 1)
+    mine = onehot(((column & (width - 1)) == me_r * BRANCHES + (node & 15)) & ((node >> 4) == column // width))
+    whither = jnp.concatenate([stacked([anc_dev[s], slot[s]], 16, width) for s in range(STEPS)], axis=1)
+    own_row = dot_nt(whither, mine)
+    own_col = dot_nt(mine, whither)
+    own_addr_row = own_row[0:1] * CAP + own_row[1:2]
+    own_addr_col = own_col[:NODES, 0:1] * CAP + own_col[:NODES, 1:2]
+    at = iota((2 * CAP * br_count, 128), 0)
+    is_node = iota((2 * CAP * br_count, 128), 1) < NODES
+    placed = is_node & ((at >> 1).astype(F32) == own_addr_row)
+    padding = jnp.zeros((128 - NODES, 640), BF)
+    queries = q_ref[...]
+    fresh_key = jnp.concatenate([fresh_ref[s, 0] for s in range(STEPS)], axis=0)
+    fresh_value = jnp.concatenate([fresh_ref[s, 1] for s in range(STEPS)], axis=0)
+    low = jnp.concatenate([jnp.concatenate([queries[:, :512], fresh_key], axis=1), padding], axis=0)
+    high = jnp.concatenate([jnp.concatenate([queries[:, 512:], fresh_value], axis=1), padding], axis=0)
+    sendm[...] = (dot(onehot(placed & ((at & 1) == 0)), low) + dot(onehot(placed & ((at & 1) == 1)), high)).astype(BF)
+
+    def message(i, source):
+        peer = peer_r(i)
+        return pltpu.make_async_remote_copy(
+            src_ref=sendm.at[pl.ds(pl.multiple_of(peer * 16, 16), 16)],
+            dst_ref=recvm.at[pl.ds(pl.multiple_of(source * 16, 16), 16)],
+            send_sem=m_send.at[peer], recv_sem=m_recv.at[source],
+            device_id={"br": peer}, device_id_type=pl.DeviceIdType.MESH)
+
+    def query_copy(i, source):
+        peer = head_at(i)
+        return pltpu.make_async_remote_copy(
+            src_ref=q_ref, dst_ref=qbuf.at[source],
+            send_sem=q_send.at[peer], recv_sem=q_recv.at[source],
+            device_id={"ctx": peer}, device_id_type=pl.DeviceIdType.MESH)
+
+    pl.semaphore_wait(barrier, ctx_count - 1 + br_count - 1)
+
+    @pl.loop(1, ctx_count)
+    def _(i):
+        query_copy(i, me_c).start()
+
+    @pl.loop(1, br_count)
+    def _(i):
+        message(i, me_r).start()
+
+    own16 = pl.ds(pl.multiple_of(me_r * 16, 16), 16)
+    recvm[own16, :] = sendm[own16, :]
+    qbuf[me_c] = queries
+
+    here = (iota((br_count, width), 0) == me_r).astype(F32)
+    home_count = jnp.sum(here * count, axis=0, keepdims=True)
+    col_at = iota((width, width), 1)
+    earlier = onehot(((row_at & 15) == 0) & ((row_at >> 4) < (col_at >> 4)))
+    ahead = dot(stacked([home_count], 16, width), earlier)[0:1]
+    home = lax.shift_right_logical(iota((1, width), 1), 4).astype(F32)
+    local_at = (iota((1, width), 1) & 15).astype(F32)
+    ones = jnp.ones((1, width), F32)
+    live_rows = iota((128, width), 0).astype(F32)
+    chosen, known = [], []
+    for s in range(STEPS):
+        arrives = anc_dev[s] == me_r.astype(F32)
+        place_at = jnp.where(arrives, ahead + slot[s] + FIRST, -1.0)
+        chosen.append(onehot(live_rows == place_at))
+        known.append(stacked([
+            ones, home, slot[s], anc_loc[s], home + 32.0 * s, local_at,
+            par_hi[s], par_lo[s], old_hi[s], old_lo[s]], 16, width))
+    chosen = jnp.concatenate(chosen, axis=1)
+    known = jnp.concatenate(known, axis=1)
+    row_info = dot_nt(known, chosen)
+    col_info = dot_nt(chosen, known)[FIRST:FIRST + LIVE]
+    addr_row = jnp.where(row_info[0:1] > 0.5, row_info[1:2] * CAP + row_info[2:3], -1.0)
+    addr_col = jnp.where(col_info[:, 0:1] > 0.5, col_info[:, 1:2] * CAP + col_info[:, 2:3], -1.0)
+    self_col = jnp.where(col_info[:, 0:1] > 0.5, col_info[:, 4:5] * 16.0 + col_info[:, 5:6], -100.0)
+    lane_live = iota((LIVE, 128), 1)
+    extra_query = onehot((lane_live.astype(F32) == col_info[:, 3:4]) | (lane_live == iota((LIVE, 128), 0) + FIRST))
+    on_path = self_col == row_info[4:5] * 16.0 + row_info[5:6]
+    on_path = on_path | (self_col == row_info[6:7] * 16.0 + row_info[7:8])
+    on_path = on_path | (self_col == row_info[8:9] * 16.0 + row_info[9:10])
+    seen = on_path | ((lane_live < FIRST) & (self_col > -1.0))
+    kcat[32, pl.ds(0, LIVE), pl.ds(128, 128)] = jnp.where(seen, 0.0, MASKED).astype(BF)
+    kcat[32, pl.ds(LIVE, 128 - LIVE), pl.ds(128, 128)] = jnp.full((128 - LIVE, 128), MASKED, BF)
+    kcat[32, pl.ds(LIVE, 128 - LIVE), pl.ds(0, 128)] = jnp.zeros((128 - LIVE, 128), BF)
+    vcat[32, pl.ds(LIVE, 128 - LIVE)] = jnp.zeros((128 - LIVE, 128), BF)
+
+    page_at = iota((32, 128), 0)
+    page_lane = iota((32, 128), 1)
+    live = jnp.where(page_lane < FIRST, 0, 128)
+    for branch in range(BRANCHES):
+        length = len_ref[me_r * BRANCHES + branch]
+        for page in range(2):
+            number = page_ref[branch, page] - me_r * 32
+            held = jnp.clip(length - 128 * page, 0, 128)
+            live = jnp.where((page_at == number) & (page_lane == branch), held, live)
+    position = iota((128, 128), 0)
+    for page in range(32):
+        kcat[page, :, pl.ds(128, 128)] = jnp.where(position < live[page:page + 1], 0.0, MASKED).astype(BF)
+
+    stat_lane = iota((NODES, 128), 1)
+
+    def part_copy(i, source):
+        peer = head_at(i)
+        return pltpu.make_async_remote_copy(
+            src_ref=part_send.at[peer], dst_ref=part_recv.at[source],
+            send_sem=p_send.at[peer], recv_sem=p_recv.at[source],
+            device_id={"ctx": peer}, device_id_type=pl.DeviceIdType.MESH)
+
+    @pl.loop(0, ctx_count)
+    def _(i):
+        g = head_at(i)
+
+        @pl.when(i > 0)
+        def _():
+            query_copy(i, g).wait_recv()
+
+        kv_copy(i, 0).wait()
+        kv_copy(i, 1).wait()
+        key = kbuf[g]
+        value = vbuf[g]
+        stat = jnp.zeros((NODES, 128), F32)
+        for half in range(2):
+            rows = jnp.concatenate(
+                [qbuf[g, :, pl.ds((4 * half + h) * 128, 128)] for h in range(4)], axis=0)
+            peak, total, summed = softmax_block(rows, key, value)
+            part_send[g, pl.ds(half * 4 * NODES, 4 * NODES)] = summed
+            for h in range(4):
+                cut = slice(h * NODES, (h + 1) * NODES)
+                stat = jnp.where(stat_lane == 4 * half + h, peak[cut], stat)
+                stat = jnp.where(stat_lane == 8 + 4 * half + h, total[cut], stat)
+        part_send[g, pl.ds(ROWS, NODES)] = stat
+
+        @pl.when(i > 0)
+        def _():
+            part_copy(i, me_c).start()
+
+    @pl.loop(1, br_count)
+    def _(i):
+        message(0, peer_r(i)).wait_recv()
+
+    gather = iota((LIVE, 2 * CAP * br_count), 1)
+    taken = (gather >> 1).astype(F32) == addr_col
+    got = recvm[...]
+    got_low = dot(onehot(taken & ((gather & 1) == 0)), got).astype(BF)
+    got_high = dot(onehot(taken & ((gather & 1) == 1)), got).astype(BF)
+    kcat[32, pl.ds(0, LIVE), pl.ds(0, 128)] = got_low[:, 512:]
+    vcat[32, pl.ds(0, LIVE)] = got_high[:, 512:]
+    for h in range(8):
+        source = got_low if h < 4 else got_high
+        qcat[h, :, pl.ds(0, 128)] = source[:, (h % 4) * 128:(h % 4 + 1) * 128]
+        qcat[h, :, pl.ds(128, 128)] = extra_query
+    key_pages.wait()
+    value_pages.wait()
+    live_lane = iota((LIVE, 128), 1)
+    suffix_out[:, pl.ds(0, FIRST)] = jnp.zeros((9, FIRST, 128), F32)
+    suffix_out[:, pl.ds(FIRST + LIVE, 128 - FIRST - LIVE)] = jnp.zeros((9, 128 - FIRST - LIVE, 128), F32)
+
+    def suffix_head(h, stat):
+        key = kcat[...].reshape(33 * 128, 256)
+        value = vcat[...].reshape(33 * 128, 128)
+        peak, total, summed = softmax_block(qcat[h], key, value)
+        suffix_out[h, pl.ds(FIRST, LIVE)] = summed
+        stat = jnp.where(live_lane == h, peak, stat)
+        return jnp.where(live_lane == 8 + h, total, stat)
+
+    suffix_out[8, pl.ds(FIRST, LIVE)] = lax.fori_loop(0, 8, suffix_head, jnp.zeros((LIVE, 128), F32))
+    back = jnp.where(iota((CAP * br_count, 128), 0).astype(F32) == addr_row, 1.0, 0.0)
+    for h in range(9):
+        ret_send[:, pl.ds(h * 128, 128)] = jnp.dot(
+            back, suffix_out[h], precision=lax.Precision.HIGHEST, preferred_element_type=F32)
+
+    def returned(i, source):
+        peer = peer_r(i)
+        return pltpu.make_async_remote_copy(
+            src_ref=ret_send.at[pl.ds(pl.multiple_of(peer * CAP, CAP), CAP)],
+            dst_ref=ret_recv.at[pl.ds(pl.multiple_of(source * CAP, CAP), CAP)],
+            send_sem=r_send.at[peer], recv_sem=r_recv.at[source],
+            device_id={"br": peer}, device_id_type=pl.DeviceIdType.MESH)
+
+    @pl.loop(1, br_count)
+    def _(i):
+        returned(i, me_r).start()
+
+    own8 = pl.ds(pl.multiple_of(me_r * CAP, CAP), CAP)
+    ret_recv[own8, :] = ret_send[own8, :]
+
+    part_recv[me_c] = part_send[me_c]
+
+    @pl.loop(1, ctx_count)
+    def _(i):
+        part_copy(0, head_at(i)).wait_recv()
+
+    stats = [part_recv[c, pl.ds(ROWS, NODES)] for c in range(8)]
+    top = functools.reduce(jnp.maximum, stats)
+    factors = [jnp.exp2((stat - top) * EXP_SCALE) for stat in stats]
+    den = jnp.zeros((NODES, 128), F32)
+    for c in range(8):
+        den = den + factors[c] * pltpu.roll(stats[c], 120, 1)
+    for h in range(8):
+        summed = jnp.zeros((NODES, 128), F32)
+        for c in range(8):
+            summed = summed + factors[c][:, h:h + 1] * part_recv[c, pl.ds(h * NODES, NODES)]
+        num[h] = summed
+
+    @pl.loop(1, br_count)
+    def _(i):
+        returned(0, peer_r(i)).wait_recv()
+
+    mine_back = jnp.where(iota((NODES, CAP * br_count), 1).astype(F32) == own_addr_col, 1.0, 0.0)
+
+    def back_home(h):
+        return jnp.dot(mine_back, ret_recv[:, pl.ds(h * 128, 128)],
+                       precision=lax.Precision.HIGHEST, preferred_element_type=F32)
+
+    suffix_stat = back_home(8)
+    overall = jnp.maximum(top, suffix_stat)
+    prompt_factor = jnp.exp2((top - overall) * EXP_SCALE)
+    suffix_factor = jnp.exp2((suffix_stat - overall) * EXP_SCALE)
+    den = prompt_factor * den + suffix_factor * pltpu.roll(suffix_stat, 120, 1)
+    for h in range(8):
+        joined = prompt_factor[:, h:h + 1] * num[h] + suffix_factor[:, h:h + 1] * back_home(h)
+        out_ref[:, pl.ds(h * 128, 128)] = (joined / den[:, h:h + 1]).astype(BF)
+
+    @pl.loop(1, ctx_count)
+    def _(i):
+        query_copy(i, me_c).wait_send()
+        part_copy(i, me_c).wait_send()
+
+    @pl.loop(1, br_count)
+    def _(i):
+        message(i, me_r).wait_send()
+        returned(i, me_r).wait_send()
+
+
+def local(
+    prompt_key_value, suffix_page_store, page_table, lengths, parents, queries, fresh_key_value
+):
+    br_count = lax.axis_size("br")
+    ctx_count = lax.axis_size("ctx")
+    vmem = pl.BlockSpec(memory_space=pltpu.VMEM)
+    smem = pl.BlockSpec(memory_space=pltpu.SMEM)
+    anywhere = pl.BlockSpec(memory_space=pl.ANY)
+    dma = pltpu.SemaphoreType.DMA
+    slots = CAP * br_count
+    out, flag = pl.pallas_call(
+        functools.partial(kernel, br_count, ctx_count),
+        out_shape=(
+            jax.ShapeDtypeStruct((NODES, 1024), BF),
+            jax.ShapeDtypeStruct((8, 128), jnp.int32),
+        ),
+        in_specs=[smem, smem, vmem, vmem, vmem, anywhere, anywhere],
+        out_specs=(vmem, vmem),
+        scratch_shapes=[
+            pltpu.VMEM((8, 2048, 128), BF),
+            pltpu.VMEM((8, 2048, 128), BF),
+            pltpu.VMEM((33, 128, 256), BF),
+            pltpu.VMEM((33, 128, 128), BF),
+            pltpu.VMEM((8, NODES, 1024), BF),
+            pltpu.VMEM((2 * slots, 640), BF),
+            pltpu.VMEM((2 * slots, 640), BF),
+            pltpu.VMEM((8, LIVE, 256), BF),
+            pltpu.VMEM((8, ROWS + NODES, 128), F32),
+            pltpu.VMEM((8, ROWS + NODES, 128), F32),
+            pltpu.VMEM((9, 128, 128), F32),
+            pltpu.VMEM((slots, 1152), F32),
+            pltpu.VMEM((slots, 1152), F32),
+            pltpu.VMEM((8, NODES, 128), F32),
+            dma((2, 8)), dma((2,)), dma((8,)), dma((8,)), dma((32,)), dma((32,)),
+            dma((8,)), dma((8,)), dma((32,)), dma((32,)),
+        ],
+        compiler_params=pltpu.CompilerParams(
+            collective_id=0, has_side_effects=True, vmem_limit_bytes=56 * 1024 * 1024
+        ),
+    )(
+        page_table, lengths, parents, queries.reshape(NODES, 1024), fresh_key_value,
+        prompt_key_value, suffix_page_store,
+    )
+    operands = (
+        prompt_key_value, suffix_page_store, page_table, lengths, parents, queries, fresh_key_value
+    )
+    return lax.cond(
+        flag[0, 0] > 0,
+        lambda *whole: general(*whole),
+        lambda *whole: out.reshape(STEPS, BRANCHES, 1024),
+        *operands,
+    )
+
+
 def solution(mesh):
     in_specs = (
         P(None, "ctx", None),

time: 469 us -> 91.6 us (0.20)
  waiting for transfers between devices: 160 us -> 0 us
  blocking collectives: 92.9 us -> 0 us
  local copies, waits for them, and re-layouts: 85.4 us -> 3.22 us
  Pallas kernels: 0 us -> 73.9 us
  other arithmetic: 62.6 us -> 0 us
  matrix products: 26 us -> 0 us
  starting transfers between devices: 23.2 us -> 0 us
    all_to_all x3 -> x0, waiting for transfers between devices: 160 us -> none  [move_suffix(): lax.all_to_all(outbound, 'br', split_axis=0, concat_axis=0, tiled=True)]
    all_gather x7 -> x0, blocking collectives: 92.9 us -> none  [the longest x6 79 us: joined_2(): gathered = jax.tree.map(lambda a: lax.all_gather(a, axis), part)]
    pallas_call x0 -> x1, Pallas kernels: none -> 73.9 us  [local(): pl.pallas_call(functools.partial(kernel, br_count, ctx_count), out_shape=...]
    add x46 -> x0, other arithmetic: 37.9 us -> none  [the longest x21 30.4 us: fold_pair(): left_stats[2] * left_weight[..., None]]
    gather x10 -> x0, local copies, waits for them, and re-layouts: 33.8 us -> none  [the longest x3 12 us: move_suffix(): return arrived.reshape((dest_count * slot_count,) + tail_shape)[incoming]]
    unnamed x107 -> x14, local copies, waits for them, and re-layouts: 28.1 us -> 2.02 us
    dot_general x12 -> x0, matrix products: 26 us -> none  [the longest x6 12.5 us: block_stats(): jnp.einsum(einsum_form, rounded, values, preferred_element_type=jnp.float32)]
    all_to_all x3 -> x0, starting transfers between devices: 22.9 us -> none  [move_suffix(): lax.all_to_all(outbound, 'br', split_axis=0, concat_axis=0, tiled=True)]
  transfers between devices with their start and end apart: 6 -> 0, of which waited for: 3 -> 0; matrix products, arithmetic and copies ran while one was open for 29% -> 0% of each run, Pallas kernels for 0% -> 0%
where the time goes in v1:
time: 91.6 us; the launch traced here: 91.4 us
  Pallas kernels  73.9 us (81%)
  between operations  14.1 us (15%)
  local copies, waits for them, and re-layouts  3.22 us (4%)
    pallas_call x1, Pallas kernels, local(): pl.pallas_call(functools.partial(kernel, br_count, ctx_count), out_shape=...  73.9 us
    unnamed x14, local copies, waits for them, and re-layouts  2.02 us

profile of v1, /device:TPU:6, one launch (start us, length us, event | category | flops | bytes accessed | tf_op | source)
XLA Modules:
  0.0 91.4 jit_solution(4481863766793875933)
XLA Ops:
  6.5 1.4 %copy.195.page_ref = s32[16,2]{1,0:T(8,128)} copy(s32[16,2]{0,1:T(2,128)} %param.17) | data formatting | bytes 256 | tf_op args[2]
  7.9 0.0 copy-start
  7.9 0.0 copy-start.7
  7.9 0.0 copy-start.10
  7.9 0.0 copy-start.27
  7.9 0.0 copy-start.28
  7.9 0.0 copy-start.36
  7.9 73.9 %shard_map.75 = (bf16[48,1024]{1,0:T(8,128)(2,1)S(1)}, s32[8,128]{1,0:T(8,128)}) custom-call(s32[16,2]{1,0:T(8,128)} %copy.195.page_ref, s32[512]{0:T(512)} %len_ref.1, s32[3,512]{1,0:T(4,128)} %par_ref.1, bf16[48,1024]{1,0:T(8,128)(2,1)} %bitcast.429, bf16[3,2,16,128]{3,2,1,0:T(8,128)(2,1)} %fresh_ref.1, bf16[2,2048,1024]{2,1,0:T(8,128)(2,1)} %pkv_ref.1, ...), custom_call_target="tpu_custom_call" | custom-call | tf_op jit(solution)/shard_map/pallas_call | solution.py:558
  81.8 1.2 %slice.72 = s32[1,1]{1,0:T(1,128)} slice(s32[8,128]{1,0:T(8,128)} %get-tuple-element.563), slice={[0:1], [0:1]} | slice | bytes 8 | tf_op jit(solution)/shard_map/slice | solution.py:595
  83.6 0.0 copy-done
  83.7 0.0 copy-done.7
  83.7 0.0 copy-done.10
  83.7 0.0 copy-done.27
  83.7 0.0 copy-done.28
  83.7 0.0 copy-done.36
  83.7 0.2 conditional.1
  83.9 0.6 copy.306
Async XLA Ops:
  7.9 75.8 %copy-start = (s32[512]{0:T(512)S(1)}, s32[512]{0:T(512)}, u32[]{:S(2)}) copy-start(s32[512]{0:T(512)} %len_ref.1) | copy-start | bytes 6148
  7.9 75.8 %copy-start.7 = (bf16[32,2,128,128]{3,2,1,0:T(8,128)(2,1)S(1)}, bf16[32,2,128,128]{3,2,1,0:T(8,128)(2,1)}, u32[]{:S(2)}) copy-start(bf16[32,2,128,128]{3,2,1,0:T(8,128)(2,1)} %pages_ref.1) | copy-start | bytes 6291460
  7.9 75.8 %copy-start.10 = (bf16[3,16,1024]{2,1,0:T(8,128)(2,1)S(1)}, bf16[3,16,1024]{2,1,0:T(8,128)(2,1)}, u32[]{:S(2)}) copy-start(bf16[3,16,1024]{2,1,0:T(8,128)(2,1)} %param.20) | copy-start | bytes 294916
  7.9 75.8 %copy-start.27 = (bf16[3,2,16,128]{3,2,1,0:T(8,128)(2,1)S(1)}, bf16[3,2,16,128]{3,2,1,0:T(8,128)(2,1)}, u32[]{:S(2)}) copy-start(bf16[3,2,16,128]{3,2,1,0:T(8,128)(2,1)} %fresh_ref.1) | copy-start | bytes 73732
  7.9 75.8 %copy-start.28 = (s32[3,512]{1,0:T(4,128)S(1)}, s32[3,512]{1,0:T(4,128)}, u32[]{:S(2)}) copy-start(s32[3,512]{1,0:T(4,128)} %par_ref.1) | copy-start | bytes 18436
  7.9 75.8 %copy-start.36 = (s32[16,2]{0,1:T(2,128)S(1)}, s32[16,2]{0,1:T(2,128)}, u32[]{:S(2)}) copy-start(s32[16,2]{0,1:T(2,128)} %param.17) | copy-start | bytes 388

commit v2 on v1

--- a/solution.py
+++ b/solution.py
@@ -228,8 +228,9 @@
     br_count, ctx_count,
     page_ref, len_ref, par_ref, q_ref, fresh_ref, pkv_ref, pages_ref,
     out_ref, flag_ref,
-    kbuf, vbuf, kcat, vcat, qbuf, sendm, recvm, qcat, part_send, part_recv, suffix_out, ret_send, ret_recv, num,
-    kv_sem, page_sem, q_send, q_recv, m_send, m_recv, p_send, p_recv, r_send, r_recv,
+    kbuf, vbuf, kcat, vcat, qbuf, sendm, recvm, qcat, part_send, part_recv, suffix_stat, code_high, code_low,
+    stat_send, stat_recv, ret_send, ret_recv, num,
+    kv_sem, page_sem, q_send, q_recv, m_send, m_recv, p_send, p_recv, r_send, r_recv, s_send, s_recv,
 ):
     me_c = lax.axis_index("ctx")
     me_r = lax.axis_index("br")
@@ -312,7 +313,7 @@
     most = jnp.max(count)
     fullest = jnp.max(jnp.sum(count, axis=1, keepdims=True)) / BRANCHES
     over = (most > CAP) | (fullest > LIVE)
-    flag_ref[...] = jnp.where(over, 1, 0) + jnp.zeros((8, 128), jnp.int32)
+    flag_ref[0, 0] = jnp.where(over, 1, 0)
 
     node = iota((128, STEPS * width), 0)
     column = iota((128, STEPS * width), 1)
@@ -403,7 +404,7 @@
     for branch in range(BRANCHES):
         length = len_ref[me_r * BRANCHES + branch]
         for page in range(2):
-            number = page_ref[branch, page] - me_r * 32
+            number = page_ref[page, branch] - me_r * 32
             held = jnp.clip(length - 128 * page, 0, 128)
             live = jnp.where((page_at == number) & (page_lane == branch), held, live)
     position = iota((128, 128), 0)
@@ -460,42 +461,70 @@
     vcat[32, pl.ds(0, LIVE)] = got_high[:, 512:]
     for h in range(8):
         source = got_low if h < 4 else got_high
-        qcat[h, :, pl.ds(0, 128)] = source[:, (h % 4) * 128:(h % 4 + 1) * 128]
-        qcat[h, :, pl.ds(128, 128)] = extra_query
+        qcat[pl.ds(h * LIVE, LIVE), pl.ds(0, 128)] = source[:, (h % 4) * 128:(h % 4 + 1) * 128]
+        qcat[pl.ds(h * LIVE, LIVE), pl.ds(128, 128)] = extra_query
     key_pages.wait()
     value_pages.wait()
     live_lane = iota((LIVE, 128), 1)
-    suffix_out[:, pl.ds(0, FIRST)] = jnp.zeros((9, FIRST, 128), F32)
-    suffix_out[:, pl.ds(FIRST + LIVE, 128 - FIRST - LIVE)] = jnp.zeros((9, 128 - FIRST - LIVE, 128), F32)
-
-    def suffix_head(h, stat):
+    lane_rows = iota((4 * LIVE, 128), 1)
+    @pl.loop(0, 2)
+    def _(part):
         key = kcat[...].reshape(33 * 128, 256)
         value = vcat[...].reshape(33 * 128, 128)
-        peak, total, summed = softmax_block(qcat[h], key, value)
-        suffix_out[h, pl.ds(FIRST, LIVE)] = summed
-        stat = jnp.where(live_lane == h, peak, stat)
-        return jnp.where(live_lane == 8 + h, total, stat)
-
-    suffix_out[8, pl.ds(FIRST, LIVE)] = lax.fori_loop(0, 8, suffix_head, jnp.zeros((LIVE, 128), F32))
-    back = jnp.where(iota((CAP * br_count, 128), 0).astype(F32) == addr_row, 1.0, 0.0)
-    for h in range(9):
-        ret_send[:, pl.ds(h * 128, 128)] = jnp.dot(
-            back, suffix_out[h], precision=lax.Precision.HIGHEST, preferred_element_type=F32)
+        rows = pl.ds(pl.multiple_of(part * 4 * LIVE, 4 * LIVE), 4 * LIVE)
+        peak, total, summed = softmax_block(qcat[rows], key, value)
+        largest = jnp.max(jnp.abs(summed), axis=1, keepdims=True)
+        unit = largest / 32767.0
+        coded = jnp.round(summed * jnp.where(largest > 0.0, 32767.0 / largest, 0.0))
+        upper = jnp.floor(coded / 256.0)
+        code_high[rows] = upper.astype(BF)
+        code_low[rows] = (coded - 256.0 * upper).astype(BF)
+        suffix_stat[rows] = jnp.where(
+            lane_rows == 0, peak, jnp.where(lane_rows == 1, total, unit))
+
+    address = addr_row[:, FIRST:FIRST + LIVE]
+    back = jnp.where(iota((CAP * br_count, LIVE), 0).astype(F32) == address, 1.0, 0.0)
+    stat = jnp.zeros((LIVE, 128), F32)
+    for h in range(8):
+        for kind in range(3):
+            stat = jnp.where(live_lane == 8 * kind + h, suffix_stat[pl.ds(h * LIVE, LIVE), kind:kind + 1], stat)
+    stat_send[...] = jnp.dot(back, stat, precision=lax.Precision.HIGHEST, preferred_element_type=F32)
+    slot_row = iota((2 * CAP * br_count, LIVE), 0)
+    held = (slot_row >> 1).astype(F32) == address
+    spread = jnp.concatenate([onehot(held & ((slot_row & 1) == half)) for half in range(2)], axis=1)
+
+    def rowed(code, h):
+        return jnp.concatenate([code[pl.ds(h * LIVE, LIVE)], code[pl.ds((h + 4) * LIVE, LIVE)]], axis=0)
+
+    for h in range(4):
+        upper = dot(spread, rowed(code_high, h))
+        lower = dot(spread, rowed(code_low, h))
+        ret_send[:, pl.ds(h * 128, 128)] = (256.0 * upper + lower).astype(jnp.int32).astype(jnp.int16)
 
     def returned(i, source):
         peer = peer_r(i)
         return pltpu.make_async_remote_copy(
-            src_ref=ret_send.at[pl.ds(pl.multiple_of(peer * CAP, CAP), CAP)],
-            dst_ref=ret_recv.at[pl.ds(pl.multiple_of(source * CAP, CAP), CAP)],
+            src_ref=ret_send.at[pl.ds(pl.multiple_of(peer * 16, 16), 16)],
+            dst_ref=ret_recv.at[pl.ds(pl.multiple_of(source * 16, 16), 16)],
             send_sem=r_send.at[peer], recv_sem=r_recv.at[source],
             device_id={"br": peer}, device_id_type=pl.DeviceIdType.MESH)
 
+    def returned_stat(i, source):
+        peer = peer_r(i)
+        return pltpu.make_async_remote_copy(
+            src_ref=stat_send.at[pl.ds(pl.multiple_of(peer * CAP, CAP), CAP)],
+            dst_ref=stat_recv.at[pl.ds(pl.multiple_of(source * CAP, CAP), CAP)],
+            send_sem=s_send.at[peer], recv_sem=s_recv.at[source],
+            device_id={"br": peer}, device_id_type=pl.DeviceIdType.MESH)
+
     @pl.loop(1, br_count)
     def _(i):
+        returned_stat(i, me_r).start()
         returned(i, me_r).start()
 
     own8 = pl.ds(pl.multiple_of(me_r * CAP, CAP), CAP)
-    ret_recv[own8, :] = ret_send[own8, :]
+    stat_recv[own8, :] = stat_send[own8, :]
+    ret_recv[own16, :] = ret_send[own16, :]
 
     part_recv[me_c] = part_send[me_c]
 
@@ -517,21 +546,26 @@
 
     @pl.loop(1, br_count)
     def _(i):
+        returned_stat(0, peer_r(i)).wait_recv()
         returned(0, peer_r(i)).wait_recv()
 
     mine_back = jnp.where(iota((NODES, CAP * br_count), 1).astype(F32) == own_addr_col, 1.0, 0.0)
-
-    def back_home(h):
-        return jnp.dot(mine_back, ret_recv[:, pl.ds(h * 128, 128)],
-                       precision=lax.Precision.HIGHEST, preferred_element_type=F32)
-
-    suffix_stat = back_home(8)
-    overall = jnp.maximum(top, suffix_stat)
+    back_stat = jnp.dot(mine_back, stat_recv[...], precision=lax.Precision.HIGHEST, preferred_element_type=F32)
+    slot_at = iota((NODES, 2 * CAP * br_count), 1)
+    mine_at = (slot_at >> 1).astype(F32) == own_addr_col
+    collect = jnp.concatenate([onehot(mine_at & ((slot_at & 1) == half)) for half in range(2)], axis=0)
+    arrived = ret_recv[...].astype(jnp.int32)
+    upper = dot(collect, (arrived >> 8).astype(F32).astype(BF))
+    lower = dot(collect, (arrived & 255).astype(F32).astype(BF))
+    coded = 256.0 * upper + lower
+    overall = jnp.maximum(top, back_stat)
     prompt_factor = jnp.exp2((top - overall) * EXP_SCALE)
-    suffix_factor = jnp.exp2((suffix_stat - overall) * EXP_SCALE)
-    den = prompt_factor * den + suffix_factor * pltpu.roll(suffix_stat, 120, 1)
+    suffix_factor = jnp.exp2((back_stat - overall) * EXP_SCALE)
+    den = prompt_factor * den + suffix_factor * pltpu.roll(back_stat, 120, 1)
+    unit = suffix_factor * pltpu.roll(back_stat, 112, 1)
     for h in range(8):
-        joined = prompt_factor[:, h:h + 1] * num[h] + suffix_factor[:, h:h + 1] * back_home(h)
+        back_home = coded[(h // 4) * NODES:(h // 4 + 1) * NODES, (h % 4) * 128:(h % 4 + 1) * 128]
+        joined = prompt_factor[:, h:h + 1] * num[h] + unit[:, h:h + 1] * back_home
         out_ref[:, pl.ds(h * 128, 128)] = (joined / den[:, h:h + 1]).astype(BF)
 
     @pl.loop(1, ctx_count)
@@ -542,6 +576,7 @@
     @pl.loop(1, br_count)
     def _(i):
         message(i, me_r).wait_send()
+        returned_stat(i, me_r).wait_send()
         returned(i, me_r).wait_send()
 
 
@@ -559,10 +594,10 @@
         functools.partial(kernel, br_count, ctx_count),
         out_shape=(
             jax.ShapeDtypeStruct((NODES, 1024), BF),
-            jax.ShapeDtypeStruct((8, 128), jnp.int32),
+            jax.ShapeDtypeStruct((1, 1), jnp.int32),
         ),
         in_specs=[smem, smem, vmem, vmem, vmem, anywhere, anywhere],
-        out_specs=(vmem, vmem),
+        out_specs=(vmem, smem),
         scratch_shapes=[
             pltpu.VMEM((8, 2048, 128), BF),
             pltpu.VMEM((8, 2048, 128), BF),
@@ -571,21 +606,25 @@
             pltpu.VMEM((8, NODES, 1024), BF),
             pltpu.VMEM((2 * slots, 640), BF),
             pltpu.VMEM((2 * slots, 640), BF),
-            pltpu.VMEM((8, LIVE, 256), BF),
+            pltpu.VMEM((8 * LIVE, 256), BF),
             pltpu.VMEM((8, ROWS + NODES, 128), F32),
             pltpu.VMEM((8, ROWS + NODES, 128), F32),
-            pltpu.VMEM((9, 128, 128), F32),
-            pltpu.VMEM((slots, 1152), F32),
-            pltpu.VMEM((slots, 1152), F32),
+            pltpu.VMEM((8 * LIVE, 128), F32),
+            pltpu.VMEM((8 * LIVE, 128), BF),
+            pltpu.VMEM((8 * LIVE, 128), BF),
+            pltpu.VMEM((slots, 128), F32),
+            pltpu.VMEM((slots, 128), F32),
+            pltpu.VMEM((2 * slots, 512), jnp.int16),
+            pltpu.VMEM((2 * slots, 512), jnp.int16),
             pltpu.VMEM((8, NODES, 128), F32),
             dma((2, 8)), dma((2,)), dma((8,)), dma((8,)), dma((32,)), dma((32,)),
-            dma((8,)), dma((8,)), dma((32,)), dma((32,)),
+            dma((8,)), dma((8,)), dma((32,)), dma((32,)), dma((32,)), dma((32,)),
         ],
         compiler_params=pltpu.CompilerParams(
             collective_id=0, has_side_effects=True, vmem_limit_bytes=56 * 1024 * 1024
         ),
     )(
-        page_table, lengths, parents, queries.reshape(NODES, 1024), fresh_key_value,
+        page_table.T, lengths, parents, queries.reshape(NODES, 1024), fresh_key_value,
         prompt_key_value, suffix_page_store,
     )
     operands = (

time: 91.6 us -> 75.3 us (0.82)
  Pallas kernels: 73.9 us -> 60.2 us
  local copies, waits for them, and re-layouts: 3.22 us -> 0.67 us
    pallas_call x1, Pallas kernels: 73.9 us -> 60.2 us  [local(): pl.pallas_call(functools.partial(kernel, br_count, ctx_count), out_shape=...]
    unnamed x14 -> x13, local copies, waits for them, and re-layouts: 2.02 us -> 0.67 us
    slice x1 -> x0, local copies, waits for them, and re-layouts: 1.19 us -> none  [local(): flag[0, 0] > 0]
where the time goes in v2:
time: 75.3 us; the launch traced here: 75.2 us
  Pallas kernels  60.2 us (80%)
  between operations  14.1 us (19%)
    pallas_call x1, Pallas kernels, local(): pl.pallas_call(functools.partial(kernel, br_count, ctx_count), out_shape=...  60.2 us

profile of v2, /device:TPU:6, one launch (start us, length us, event | category | flops | bytes accessed | tf_op | source)
XLA Modules:
  0.0 75.2 jit_solution(17459682871595683013)
XLA Ops:
  6.5 0.0 copy-start
  6.5 0.0 copy-start.7
  6.5 0.0 copy-start.10
  6.5 0.0 copy-start.27
  6.5 0.0 copy-start.28
  6.5 0.0 copy-start.36
  6.6 60.2 %shard_map.75 = (bf16[48,1024]{1,0:T(8,128)(2,1)S(1)}, s32[1,1]{1,0:T(1,128)}) custom-call(s32[2,16]{1,0:T(2,128)} %bitcast.447, s32[512]{0:T(512)} %len_ref.1, s32[3,512]{1,0:T(4,128)} %par_ref.1, bf16[48,1024]{1,0:T(8,128)(2,1)} %bitcast.430, bf16[3,2,16,128]{3,2,1,0:T(8,128)(2,1)} %fresh_ref.1, bf16[2,2048,1024]{2,1,0:T(8,128)(2,1)} %pkv_ref.1, ...), custom_call_target="tpu_custom_call" | custom-call | tf_op jit(solution)/shard_map/pallas_call | solution.py:593
  67.4 0.0 copy-done
  67.4 0.0 copy-done.7
  67.4 0.0 copy-done.10
  67.4 0.0 copy-done.27
  67.4 0.0 copy-done.28
  67.5 0.0 copy-done.36
  67.5 0.2 conditional.1
  67.7 0.6 copy.301
Async XLA Ops:
  6.5 60.9 %copy-start = (s32[512]{0:T(512)S(1)}, s32[512]{0:T(512)}, u32[]{:S(2)}) copy-start(s32[512]{0:T(512)} %len_ref.1) | copy-start | bytes 6148
  6.5 60.9 %copy-start.7 = (bf16[32,2,128,128]{3,2,1,0:T(8,128)(2,1)S(1)}, bf16[32,2,128,128]{3,2,1,0:T(8,128)(2,1)}, u32[]{:S(2)}) copy-start(bf16[32,2,128,128]{3,2,1,0:T(8,128)(2,1)} %pages_ref.1) | copy-start | bytes 6291460
  6.5 60.9 %copy-start.10 = (bf16[3,16,1024]{2,1,0:T(8,128)(2,1)S(1)}, bf16[3,16,1024]{2,1,0:T(8,128)(2,1)}, u32[]{:S(2)}) copy-start(bf16[3,16,1024]{2,1,0:T(8,128)(2,1)} %param.20) | copy-start | bytes 294916
  6.5 60.9 %copy-start.27 = (bf16[3,2,16,128]{3,2,1,0:T(8,128)(2,1)S(1)}, bf16[3,2,16,128]{3,2,1,0:T(8,128)(2,1)}, u32[]{:S(2)}) copy-start(bf16[3,2,16,128]{3,2,1,0:T(8,128)(2,1)} %fresh_ref.1) | copy-start | bytes 73732
  6.5 60.9 %copy-start.28 = (s32[3,512]{1,0:T(4,128)S(1)}, s32[3,512]{1,0:T(4,128)}, u32[]{:S(2)}) copy-start(s32[3,512]{1,0:T(4,128)} %par_ref.1) | copy-start | bytes 18436
  6.5 60.9 %copy-start.36 = (s32[16,2]{0,1:T(2,128)S(1)}, s32[16,2]{0,1:T(2,128)}, u32[]{:S(2)}) copy-start(s32[16,2]{0,1:T(2,128)} %param.17) | copy-start | bytes 388

commit v3 on v0

--- a/solution.py
+++ b/solution.py
@@ -1,8 +1,11 @@
+import functools
 import math
 
 import jax
 import jax.numpy as jnp
 from jax import lax
+from jax.experimental import pallas as pl
+from jax.experimental.pallas import tpu as pltpu
 from jax.sharding import PartitionSpec as P
 
 QUERY_HEADS = 64
@@ -94,7 +97,7 @@
     )
 
 
-def local(
+def general(
     prompt_key_value, suffix_page_store, page_table, lengths, parents, queries, fresh_key_value
 ):
     br_count = lax.axis_size("br")
@@ -174,6 +177,598 @@
     return jnp.stack(outputs)
 
 
+STEPS = 3
+BRANCHES = 16
+NODES = STEPS * BRANCHES
+CAP = 8
+QUAD = 4
+LIVE = 96
+LATE = 16
+ROWS = 8 * NODES
+MASKED = -1e30
+EXP_SCALE = math.log2(math.e) / math.sqrt(HEAD_SIZE)
+BF = jnp.bfloat16
+F32 = jnp.float32
+NT = (((1,), (1,)), ((), ()))
+
+
+def onehot(condition):
+    return jnp.where(condition, 1.0, 0.0).astype(BF)
+
+
+def iota(shape, axis):
+    return lax.broadcasted_iota(jnp.int32, shape, axis)
+
+
+def stacked(rows, count, width):
+    at = iota((count, width), 0)
+    out = jnp.zeros((count, width), F32)
+    for index, row in enumerate(rows):
+        out = jnp.where(at == index, row.astype(F32), out)
+    return out.astype(BF)
+
+
+def dot(left, right):
+    return jnp.dot(left, right, preferred_element_type=F32)
+
+
+def dot_nt(left, right):
+    return lax.dot_general(left, right, NT, preferred_element_type=F32)
+
+
+def softmax_block(query, key, value):
+    raw = dot_nt(query, key)
+    peak = jnp.max(raw, axis=1, keepdims=True)
+    weight = jnp.exp2((raw - peak) * EXP_SCALE)
+    total = jnp.sum(weight, axis=1, keepdims=True)
+    return peak, total, dot(weight.astype(BF), value)
+
+
+def kernel(
+    br_count, ctx_count,
+    page_ref, len_ref, par_ref, q_ref, fresh_ref, pkv_ref, pages_ref,
+    out_ref, flag_ref,
+    kbuf, vbuf, kpage, vpage, qbuf, send_a, recv_a, send_b, recv_b, qrows, part_send, part_recv,
+    code_high, code_low, late_high, late_low, stat_send, stat_recv, ret_send, ret_recv, num,
+    kv_sem, g_send, g_recv, page_sem, q_send, q_recv, a_send, a_recv, b_send, b_recv, p_send, p_recv,
+    r_send, r_recv, s_send, s_recv,
+):
+    me_c = lax.axis_index("ctx")
+    me_r = lax.axis_index("br")
+
+    core = lax.rem(me_c, 2)
+    chip = me_c // 2
+    chips = ctx_count // 2
+    partner = me_c + 1 - 2 * core
+
+    def peer_r(i):
+        return lax.rem(me_r + i, br_count)
+
+    def chip_at(t):
+        return lax.rem(chip + t, chips)
+
+    barrier = pltpu.get_barrier_semaphore()
+
+    @pl.loop(1, chips)
+    def _(t):
+        pl.semaphore_signal(
+            barrier, inc=1, device_id={"ctx": chip_at(t) * 2 + core}, device_id_type=pl.DeviceIdType.MESH)
+
+    pl.semaphore_signal(barrier, inc=1, device_id={"ctx": partner}, device_id_type=pl.DeviceIdType.MESH)
+
+    @pl.loop(1, br_count)
+    def _(i):
+        pl.semaphore_signal(barrier, inc=1, device_id={"br": peer_r(i)}, device_id_type=pl.DeviceIdType.MESH)
+
+    def head_columns(t, parity):
+        return pl.ds(pl.multiple_of((chip_at(t) * 2 + parity) * HEAD_SIZE, HEAD_SIZE), HEAD_SIZE)
+
+    def kv_copy(t, which):
+        buffer = kbuf if which == 0 else vbuf
+        return pltpu.make_async_copy(
+            pkv_ref.at[which, :, head_columns(t, core)], buffer.at[t, 0], kv_sem.at[which, t])
+
+    def kv_give(t, which):
+        buffer = kbuf if which == 0 else vbuf
+        return pltpu.make_async_remote_copy(
+            src_ref=pkv_ref.at[which, :, head_columns(t, 1 - core)], dst_ref=buffer.at[t, 1],
+            send_sem=g_send.at[which, t], recv_sem=g_recv.at[which, t],
+            device_id={"ctx": partner}, device_id_type=pl.DeviceIdType.MESH)
+
+    key_pages = pltpu.make_async_copy(pages_ref.at[:, 0], kpage, page_sem.at[0])
+    value_pages = pltpu.make_async_copy(pages_ref.at[:, 1], vpage, page_sem.at[1])
+
+    @pl.loop(0, chips)
+    def _(t):
+        kv_copy(t, 0).start()
+        kv_copy(t, 1).start()
+
+    key_pages.start()
+    value_pages.start()
+
+    parent = par_ref[...]
+    device = lax.shift_right_logical(parent, 4)
+    place = parent & 15
+    width = parent.shape[1]
+    row_at = iota((width, width), 0)
+    pick1 = onehot(row_at == parent[1:2])
+    pick2 = onehot(row_at == parent[2:3])
+    first = dot(stacked([device[0:1], place[0:1]], 16, width), pick1)
+    second = dot(stacked([first[0:1], first[1:2], device[1:2], place[1:2]], 16, width), pick2)
+    anc_dev = [device[0:1].astype(F32), first[0:1], second[0:1]]
+    anc_loc = [place[0:1].astype(F32), first[1:2], second[1:2]]
+    missing = jnp.full((1, width), -1.0, F32)
+    par_hi = [missing, device[1:2].astype(F32), device[2:3].astype(F32) + 32.0]
+    par_lo = [missing, place[1:2].astype(F32), place[2:3].astype(F32)]
+    old_hi = [missing, missing, second[2:3]]
+    old_lo = [missing, missing, second[3:4]]
+
+    owner = iota((br_count, width), 0).astype(F32)
+    to_owner = [onehot(owner == anc_dev[s]) for s in range(STEPS)]
+    j = iota((128, 256), 0)
+    lane = iota((128, 256), 1)
+    b = lane & 127
+    same_home = (j >> 4) == (b >> 4)
+    counting = onehot(same_home & ((lane >= 128) | (j < b)))
+    slots = [[], [], []]
+    pair_count = []
+    for tile in range(width // 128):
+        cut = [m[:, tile * 128:(tile + 1) * 128] for m in to_owner]
+        counted = dot(jnp.concatenate(cut, axis=0), counting)
+        before = jnp.zeros((br_count, 128), F32)
+        for s in range(STEPS):
+            block = counted[s * br_count:(s + 1) * br_count]
+            slots[s].append(jnp.sum(cut[s].astype(F32) * (block[:, :128] + before), axis=0, keepdims=True))
+            before = before + block[:, 128:]
+        pair_count.append(before)
+    slot = [jnp.concatenate(parts, axis=1) for parts in slots]
+    count = jnp.concatenate(pair_count, axis=1)
+    most = jnp.max(count)
+    first_count = jnp.minimum(count, QUAD)
+    fullest = jnp.max(jnp.sum(first_count, axis=1, keepdims=True)) / BRANCHES
+    latest = jnp.max(jnp.sum(count - first_count, axis=1, keepdims=True)) / BRANCHES
+    over = (most > CAP) | (fullest > LIVE) | (latest > LATE)
+    flag_ref[0, 0] = jnp.where(over, 1, 0)
+
+    node = iota((128, STEPS * width), 0)
+    column = iota((128, STEPS * width), 1)
+    mine = onehot(((column & (width - 1)) == me_r * BRANCHES + (node & 15)) & ((node >> 4) == column // width))
+    whither = jnp.concatenate([stacked([anc_dev[s], slot[s]], 16, width) for s in range(STEPS)], axis=1)
+    own_row = dot_nt(whither, mine)
+    own_col = dot_nt(mine, whither)
+    own_dev, own_slot = own_col[:NODES, 0:1], own_col[:NODES, 1:2]
+    at = iota((16 * br_count, 128), 0)
+    is_node = iota((16 * br_count, 128), 1) < NODES
+    own_pair = is_node & ((at >> 1).astype(F32) == own_row[0:1] * CAP + own_row[1:2])
+    quad_row = own_row[0:1] * QUAD + own_row[1:2]
+    own_first = is_node & (own_row[1:2] < QUAD) & ((at >> 2).astype(F32) == quad_row)
+    own_late = is_node & (own_row[1:2] >= QUAD) & ((at >> 2).astype(F32) == quad_row - QUAD)
+    queries = q_ref[...]
+
+    def padded(rows):
+        return jnp.concatenate([rows, jnp.zeros((128 - NODES, rows.shape[1]), BF)], axis=0)
+
+    fresh = [padded(jnp.concatenate([fresh_ref[s, kind] for s in range(STEPS)], axis=0)) for kind in range(2)]
+    quarters = jnp.concatenate([padded(queries[:, 256 * n:256 * (n + 1)]) for n in range(4)], axis=0)
+
+    def spread_over(rows, parts, mask):
+        return jnp.concatenate([onehot(mask & ((rows & (parts - 1)) == part)) for part in range(parts)], axis=1)
+
+    send_a[:, pl.ds(0, 256)] = dot(spread_over(at, 4, own_first), quarters).astype(BF)
+    send_a[:, pl.ds(256, 128)] = dot(spread_over(at, 2, own_pair), jnp.concatenate(fresh, axis=0)).astype(BF)
+    send_b[...] = dot(spread_over(at, 4, own_late), quarters).astype(BF)
+
+    def rows16(index):
+        return pl.ds(pl.multiple_of(index * 16, 16), 16)
+
+    def to_br(i, source, send, recv, send_sem, recv_sem):
+        peer = peer_r(i)
+        return pltpu.make_async_remote_copy(
+            src_ref=send.at[rows16(peer)], dst_ref=recv.at[rows16(source)],
+            send_sem=send_sem.at[peer], recv_sem=recv_sem.at[source],
+            device_id={"br": peer}, device_id_type=pl.DeviceIdType.MESH)
+
+    def message_a(i, source):
+        return to_br(i, source, send_a, recv_a, a_send, a_recv)
+
+    def message_b(i, source):
+        return to_br(i, source, send_b, recv_b, b_send, b_recv)
+
+    def query_copy(t, source):
+        return pltpu.make_async_remote_copy(
+            src_ref=q_ref, dst_ref=qbuf.at[source],
+            send_sem=q_send.at[t], recv_sem=q_recv.at[source],
+            device_id={"ctx": chip_at(t) * 2 + core}, device_id_type=pl.DeviceIdType.MESH)
+
+    pl.semaphore_wait(barrier, chips + br_count - 1)
+
+    @pl.loop(1, chips)
+    def _(t):
+        query_copy(t, chip).start()
+        kv_give(t, 0).start()
+        kv_give(t, 1).start()
+
+    kv_give(0, 0).start()
+    kv_give(0, 1).start()
+
+    @pl.loop(1, br_count)
+    def _(i):
+        message_a(i, me_r).start()
+
+    @pl.loop(1, br_count)
+    def _(i):
+        message_b(i, me_r).start()
+
+    own16 = rows16(me_r)
+    recv_a[own16, :] = send_a[own16, :]
+    recv_b[own16, :] = send_b[own16, :]
+    qbuf[chip] = queries
+
+    here = (iota((br_count, width), 0) == me_r).astype(F32)
+    home_count = jnp.sum(here * count, axis=0, keepdims=True)
+    col_at = iota((width, width), 1)
+    earlier = onehot(((row_at & 15) == 0) & ((row_at >> 4) < (col_at >> 4)))
+    home_first = jnp.minimum(home_count, QUAD)
+    ahead = dot(stacked([home_first, home_count - home_first], 16, width), earlier)
+    home = lax.shift_right_logical(iota((1, width), 1), 4).astype(F32)
+    local_at = (iota((1, width), 1) & 15).astype(F32)
+    ones = jnp.ones((1, width), F32)
+    live_rows = iota((128, width), 0).astype(F32)
+    chosen, known = [], []
+    for s in range(STEPS):
+        arrives = anc_dev[s] == me_r.astype(F32)
+        first_at = ahead[0:1] + slot[s]
+        late_at = ahead[1:2] + slot[s] - QUAD
+        late_at = jnp.where((slot[s] < CAP) & (late_at < LATE), late_at + LIVE, -1.0)
+        place_at = jnp.where(slot[s] < QUAD, jnp.where(first_at < LIVE, first_at, -1.0), late_at)
+        place_at = jnp.where(arrives, place_at, -1.0)
+        chosen.append(onehot(live_rows == place_at))
+        known.append(stacked([
+            ones, home, slot[s], anc_loc[s], home + 32.0 * s, local_at,
+            par_hi[s], par_lo[s], old_hi[s], old_lo[s]], 16, width))
+    chosen = jnp.concatenate(chosen, axis=1)
+    known = jnp.concatenate(known, axis=1)
+    row_info = dot_nt(known, chosen)
+    col_info = dot_nt(chosen, known)
+    here_row = row_info[0:1] > 0.5
+    here_col = col_info[:, 0:1] > 0.5
+    slot_row, slot_col = row_info[2:3], col_info[:, 2:3]
+    pair_col = jnp.where(here_col, col_info[:, 1:2] * CAP + slot_col, -1.0)
+    quad_col = jnp.where(here_col, col_info[:, 1:2] * QUAD + slot_col, -1.0)
+    quad_row = jnp.where(here_row, row_info[1:2] * QUAD + slot_row, -1.0)
+    self_row = jnp.where(here_row, row_info[4:5] * 16.0 + row_info[5:6], -100.0)
+    on_path = self_row == col_info[:, 4:5] * 16.0 + col_info[:, 5:6]
+    on_path = on_path | (self_row == col_info[:, 6:7] * 16.0 + col_info[:, 7:8])
+    on_path = on_path | (self_row == col_info[:, 8:9] * 16.0 + col_info[:, 9:10])
+    path = jnp.where(on_path, 1.0, 0.0)
+    anc_col = col_info[:, 3:4]
+    length_col = jnp.zeros((128, 1), F32)
+    for branch in range(BRANCHES):
+        length_col = jnp.where(anc_col == branch, len_ref[me_r * BRANCHES + branch].astype(F32), length_col)
+
+    stat_lane = iota((NODES, 128), 1)
+
+    def part_copy(t, source):
+        peer = chip_at(t)
+        return pltpu.make_async_remote_copy(
+            src_ref=part_send.at[peer], dst_ref=part_recv.at[source],
+            send_sem=p_send.at[peer], recv_sem=p_recv.at[source],
+            device_id={"ctx": peer * 2 + core}, device_id_type=pl.DeviceIdType.MESH)
+
+    def prompt_block(t, block):
+        where = chip_at(t)
+        if block == 0:
+            kv_copy(t, 0).wait()
+            kv_copy(t, 1).wait()
+        else:
+            kv_give(t, 0).wait_recv()
+            kv_give(t, 1).wait_recv()
+        key = kbuf[t, block]
+        value = vbuf[t, block]
+        old = part_send[where, pl.ds(ROWS, NODES)]
+        stat = jnp.zeros((NODES, 128), F32)
+        for half in range(2):
+            heads = range(4 * half, 4 * half + 4)
+            rows = jnp.concatenate([qbuf[where, :, pl.ds(h * 128, 128)] for h in heads], axis=0)
+            peak, total, summed = softmax_block(rows, key, value)
+            part = pl.ds(half * 4 * NODES, 4 * NODES)
+            if block == 1:
+                old_peak = jnp.concatenate([old[:, h:h + 1] for h in heads], axis=0)
+                old_total = jnp.concatenate([old[:, 8 + h:9 + h] for h in heads], axis=0)
+                joint = jnp.maximum(peak, old_peak)
+                old_factor = jnp.exp2((old_peak - joint) * EXP_SCALE)
+                factor = jnp.exp2((peak - joint) * EXP_SCALE)
+                total = old_factor * old_total + factor * total
+                summed = old_factor * part_send[where, part] + factor * summed
+                peak = joint
+            part_send[where, part] = summed
+            for h in heads:
+                cut = slice((h - 4 * half) * NODES, (h - 4 * half + 1) * NODES)
+                stat = jnp.where(stat_lane == h, peak[cut], stat)
+                stat = jnp.where(stat_lane == 8 + h, total[cut], stat)
+        part_send[where, pl.ds(ROWS, NODES)] = stat
+
+    prompt_block(0, 0)
+
+    @pl.loop(1, chips)
+    def _(t):
+        query_copy(t, chip_at(t)).wait_recv()
+        prompt_block(t, 0)
+        prompt_block(t, 1)
+        part_copy(t, chip).start()
+
+    @pl.loop(1, br_count)
+    def _(i):
+        message_a(0, peer_r(i)).wait_recv()
+
+    got_a = recv_a[...]
+    gather = iota((128, 16 * br_count), 1)
+    pairs = (gather >> 1).astype(F32) == pair_col
+    new_key = dot(onehot(pairs & ((gather & 1) == 0)), got_a[:, 256:]).astype(BF)
+    new_value = dot(onehot(pairs & ((gather & 1) == 1)), got_a[:, 256:]).astype(BF)
+
+    def gathered(address, got):
+        count = address.shape[0]
+        place = iota((count, 16 * br_count), 1)
+        match = (place >> 2).astype(F32) == address
+        parts = jnp.concatenate([onehot(match & ((place & 3) == part)) for part in range(4)], axis=0)
+        return dot(parts, got).astype(BF)
+
+    taken = gathered(quad_col[:LIVE], got_a[:, :256])
+    for n in range(4):
+        for half in range(2):
+            qrows[n, pl.ds(half * LIVE, LIVE)] = taken[n * LIVE:(n + 1) * LIVE, half * 128:(half + 1) * 128]
+    key_pages.wait()
+    value_pages.wait()
+
+    def suffix_block(rows, anc, length, see):
+        count = rows.shape[0]
+        fold = jnp.zeros((count, 256), F32)
+        for branch in range(BRANCHES):
+            key = jnp.concatenate([kpage[lax.rem(page_ref[page, branch], 32)] for page in range(2)], axis=0)
+            fold = jnp.where(anc == branch, dot_nt(rows, key), fold)
+        fold = jnp.where(iota((count, 256), 1).astype(F32) < length, fold, MASKED)
+        new = jnp.where(see > 0.5, dot_nt(rows, new_key), MASKED)
+        peak = jnp.maximum(jnp.max(fold, axis=1, keepdims=True), jnp.max(new, axis=1, keepdims=True))
+        weight = jnp.exp2((fold - peak) * EXP_SCALE)
+        new = jnp.exp2((new - peak) * EXP_SCALE)
+        total = jnp.sum(weight, axis=1, keepdims=True) + jnp.sum(new, axis=1, keepdims=True)
+        weight = weight.astype(BF)
+        summed = dot(new.astype(BF), new_value)
+        for branch in range(0, BRANCHES, 2):
+            value = jnp.concatenate([jnp.concatenate(
+                [vpage[lax.rem(page_ref[page, b], 32)] for page in range(2)], axis=0)
+                for b in (branch, branch + 1)], axis=1)
+            both = dot(weight, value)
+            summed = jnp.where(anc == branch, summed + both[:, :128], summed)
+            summed = jnp.where(anc == branch + 1, summed + both[:, 128:], summed)
+        largest = jnp.max(jnp.abs(summed), axis=1, keepdims=True)
+        coded = jnp.round(summed * jnp.where(largest > 0.0, 32767.0 / largest, 0.0))
+        upper = jnp.floor(coded / 256.0)
+        sum_log = peak * EXP_SCALE + jnp.log2(total)
+        return upper.astype(BF), (coded - 256.0 * upper).astype(BF), sum_log, largest / (32767.0 * total)
+
+    def repeated(column, times):
+        return jnp.concatenate([column] * times, axis=0)
+
+    def stat_rows(stat, cut):
+        lane = iota(stat.shape, 1)
+        stat = jnp.where((lane >> 4).astype(F32) == slot_col[cut], stat, 0.0)
+        home_at = iota((br_count, stat.shape[0]), 0).astype(F32)
+        own_home = jnp.where(here_row[:, cut] & (home_at == row_info[1:2, cut]), 1.0, 0.0)
+        return jnp.dot(own_home, stat, precision=lax.Precision.HIGHEST, preferred_element_type=F32)
+
+    def return_rows(address, high, low):
+        count = address.shape[1]
+        rows = iota((16 * br_count, count), 0)
+        spread = spread_over(rows, 4, (rows >> 2).astype(F32) == address)
+        return (256.0 * dot(spread, high) + dot(spread, low)).astype(jnp.int32).astype(jnp.int16)
+
+    def returned(group, i, source):
+        return to_br(i, source, ret_send.at[group], ret_recv.at[group], r_send.at[group], r_recv.at[group])
+
+    def returned_stat(group, i, source):
+        peer = peer_r(i)
+        return pltpu.make_async_remote_copy(
+            src_ref=stat_send.at[group, peer], dst_ref=stat_recv.at[group, source],
+            send_sem=s_send.at[group, peer], recv_sem=s_recv.at[group, source],
+            device_id={"br": peer}, device_id_type=pl.DeviceIdType.MESH)
+
+    def give_back(group, stat, rows):
+        for home_index in range(br_count):
+            stat_send[group, home_index] = stat[home_index:home_index + 1]
+        ret_send[group] = rows
+
+        @pl.loop(1, br_count)
+        def _(i):
+            returned_stat(group, i, me_r).start()
+            returned(group, i, me_r).start()
+
+        stat_recv[group, me_r] = stat_send[group, me_r]
+        ret_recv[group, own16, :] = ret_send[group, own16, :]
+
+    first_lane = iota((LIVE, 128), 1) & 15
+
+    def suffix_quarter(n, stat):
+        high, low, sum_log, unit = suffix_block(
+            qrows[n], repeated(anc_col[:LIVE], 2), repeated(length_col[:LIVE], 2), repeated(path[:LIVE], 2))
+        quarter = pl.ds(pl.multiple_of(n * LIVE, LIVE), LIVE)
+        for half in range(2):
+            cut = slice(half * LIVE, (half + 1) * LIVE)
+            code_high[quarter, pl.ds(half * 128, 128)] = high[cut]
+            code_low[quarter, pl.ds(half * 128, 128)] = low[cut]
+            stat = jnp.where(first_lane == 2 * n + half, sum_log[cut], stat)
+            stat = jnp.where(first_lane == 8 + 2 * n + half, unit[cut], stat)
+        return stat
+
+    stat_a = lax.fori_loop(0, 4, suffix_quarter, jnp.zeros((LIVE, 128), F32))
+
+    give_back(0, stat_rows(stat_a, slice(0, LIVE)),
+              return_rows(quad_row[:, :LIVE], code_high[...], code_low[...]))
+
+    prompt_block(0, 1)
+
+    @pl.loop(1, br_count)
+    def _(i):
+        message_b(0, peer_r(i)).wait_recv()
+
+    late = slice(LIVE, LIVE + LATE)
+    taken = gathered(quad_col[late] - QUAD, recv_b[...])
+    rows = jnp.concatenate([
+        taken[(h // 2) * LATE:(h // 2 + 1) * LATE, (h % 2) * 128:(h % 2 + 1) * 128] for h in range(8)], axis=0)
+    high, low, sum_log, unit = suffix_block(
+        rows, repeated(anc_col[late], 8), repeated(length_col[late], 8), repeated(path[late], 8))
+    late_lane = iota((LATE, 128), 1) & 15
+    stat_b = jnp.zeros((LATE, 128), F32)
+    for h in range(8):
+        cut = slice(h * LATE, (h + 1) * LATE)
+        late_high[pl.ds((h // 2) * LATE, LATE), pl.ds((h % 2) * 128, 128)] = high[cut]
+        late_low[pl.ds((h // 2) * LATE, LATE), pl.ds((h % 2) * 128, 128)] = low[cut]
+        stat_b = jnp.where(late_lane == h, sum_log[cut], stat_b)
+        stat_b = jnp.where(late_lane == 8 + h, unit[cut], stat_b)
+    give_back(1, stat_rows(stat_b, late),
+              return_rows(quad_row[:, late] - QUAD, late_high[...], late_low[...]))
+
+    part_recv[chip] = part_send[chip]
+
+    @pl.loop(1, chips)
+    def _(t):
+        part_copy(t, chip_at(t)).wait_recv()
+
+    stats = [part_recv[c, pl.ds(ROWS, NODES)] for c in range(4)]
+    top = functools.reduce(jnp.maximum, stats)
+    factors = [jnp.exp2((stat - top) * EXP_SCALE) for stat in stats]
+    den = jnp.zeros((NODES, 128), F32)
+    for c in range(4):
+        den = den + factors[c] * pltpu.roll(stats[c], 120, 1)
+    for h in range(8):
+        summed = jnp.zeros((NODES, 128), F32)
+        for c in range(4):
+            summed = summed + factors[c][:, h:h + 1] * part_recv[c, pl.ds(h * NODES, NODES)]
+        num[h] = summed
+
+    back_low = iota((4 * NODES, 16 * br_count), 1)
+    address = repeated(own_dev * QUAD + own_slot, 4)
+    quarter_at = iota((4 * NODES, 16 * br_count), 0) // NODES
+
+    def collected(group, match):
+        collect = onehot(match & ((back_low & 3) == quarter_at))
+        arrived = ret_recv[group].astype(jnp.int32)
+        upper = dot(collect, (arrived >> 8).astype(F32).astype(BF))
+        return 256.0 * upper + dot(collect, (arrived & 255).astype(F32).astype(BF))
+
+    in_first = repeated(own_slot, 4) < QUAD
+    quad_at = (back_low >> 2).astype(F32)
+
+    @pl.loop(1, br_count)
+    def _(i):
+        returned_stat(0, 0, peer_r(i)).wait_recv()
+        returned(0, 0, peer_r(i)).wait_recv()
+
+    coded = collected(0, in_first & (quad_at == address))
+
+    @pl.loop(1, br_count)
+    def _(i):
+        returned_stat(1, 0, peer_r(i)).wait_recv()
+        returned(1, 0, peer_r(i)).wait_recv()
+
+    coded = coded + collected(1, jnp.logical_not(in_first) & (quad_at == address - QUAD))
+    from_device = jnp.where(iota((NODES, br_count), 1).astype(F32) == own_dev, 1.0, 0.0)
+    all_stat = jnp.concatenate([stat_recv[0, d] + stat_recv[1, d] for d in range(br_count)], axis=0)
+    back_stat = jnp.dot(from_device, all_stat, precision=lax.Precision.HIGHEST, preferred_element_type=F32)
+    back_stat = jnp.where((stat_lane >> 4).astype(F32) == own_slot, back_stat, 0.0)
+    for shift in (64, 32, 16):
+        back_stat = back_stat + pltpu.roll(back_stat, shift, 1)
+    prompt_log = top * EXP_SCALE
+    overall = jnp.maximum(prompt_log, back_stat)
+    prompt_factor = jnp.exp2(prompt_log - overall)
+    suffix_factor = jnp.exp2(back_stat - overall)
+    den = prompt_factor * den + suffix_factor
+    unit = suffix_factor * pltpu.roll(back_stat, 120, 1)
+    for h in range(8):
+        back_home = coded[(h // 2) * NODES:(h // 2 + 1) * NODES, (h % 2) * 128:(h % 2 + 1) * 128]
+        joined = prompt_factor[:, h:h + 1] * num[h] + unit[:, h:h + 1] * back_home
+        out_ref[:, pl.ds(h * 128, 128)] = (joined / den[:, h:h + 1]).astype(BF)
+
+    @pl.loop(1, chips)
+    def _(t):
+        query_copy(t, chip).wait_send()
+        part_copy(t, chip).wait_send()
+
+    @pl.loop(0, chips)
+    def _(t):
+        kv_give(t, 0).wait_send()
+        kv_give(t, 1).wait_send()
+
+    @pl.loop(1, br_count)
+    def _(i):
+        message_a(i, me_r).wait_send()
+        message_b(i, me_r).wait_send()
+        for group in range(2):
+            returned_stat(group, i, me_r).wait_send()
+            returned(group, i, me_r).wait_send()
+
+
+def local(
+    prompt_key_value, suffix_page_store, page_table, lengths, parents, queries, fresh_key_value
+):
+    br_count = lax.axis_size("br")
+    ctx_count = lax.axis_size("ctx")
+    vmem = pl.BlockSpec(memory_space=pltpu.VMEM)
+    smem = pl.BlockSpec(memory_space=pltpu.SMEM)
+    anywhere = pl.BlockSpec(memory_space=pl.ANY)
+    dma = pltpu.SemaphoreType.DMA
+    out, flag = pl.pallas_call(
+        functools.partial(kernel, br_count, ctx_count),
+        out_shape=(
+            jax.ShapeDtypeStruct((NODES, 1024), BF),
+            jax.ShapeDtypeStruct((1, 1), jnp.int32),
+        ),
+        in_specs=[smem, smem, vmem, vmem, vmem, anywhere, anywhere],
+        out_specs=(vmem, smem),
+        scratch_shapes=[
+            pltpu.VMEM((4, 2, 2048, 128), BF),
+            pltpu.VMEM((4, 2, 2048, 128), BF),
+            pltpu.VMEM((32, 128, 128), BF),
+            pltpu.VMEM((32, 128, 128), BF),
+            pltpu.VMEM((4, NODES, 1024), BF),
+            pltpu.VMEM((16 * br_count, 384), BF),
+            pltpu.VMEM((16 * br_count, 384), BF),
+            pltpu.VMEM((16 * br_count, 256), BF),
+            pltpu.VMEM((16 * br_count, 256), BF),
+            pltpu.VMEM((4, 2 * LIVE, 128), BF),
+            pltpu.VMEM((4, ROWS + NODES, 128), F32),
+            pltpu.VMEM((4, ROWS + NODES, 128), F32),
+            pltpu.VMEM((4 * LIVE, 256), BF),
+            pltpu.VMEM((4 * LIVE, 256), BF),
+            pltpu.VMEM((4 * LATE, 256), BF),
+            pltpu.VMEM((4 * LATE, 256), BF),
+            pltpu.VMEM((2, br_count, 1, 128), F32),
+            pltpu.VMEM((2, br_count, 1, 128), F32),
+            pltpu.VMEM((2, 16 * br_count, 256), jnp.int16),
+            pltpu.VMEM((2, 16 * br_count, 256), jnp.int16),
+            pltpu.VMEM((8, NODES, 128), F32),
+            dma((2, 4)), dma((2, 4)), dma((2, 4)), dma((2,)), dma((4,)), dma((4,)), dma((32,)), dma((32,)), dma((32,)), dma((32,)),
+            dma((4,)), dma((4,)), dma((2, 32)), dma((2, 32)), dma((2, 32)), dma((2, 32)),
+        ],
+        compiler_params=pltpu.CompilerParams(
+            collective_id=0, has_side_effects=True, vmem_limit_bytes=56 * 1024 * 1024
+        ),
+    )(
+        page_table.T, lengths, parents, queries.reshape(NODES, 1024), fresh_key_value,
+        prompt_key_value, suffix_page_store,
+    )
+    operands = (
+        prompt_key_value, suffix_page_store, page_table, lengths, parents, queries, fresh_key_value
+    )
+    return lax.cond(
+        flag[0, 0] > 0,
+        lambda *whole: general(*whole),
+        lambda *whole: out.reshape(STEPS, BRANCHES, 1024),
+        *operands,
+    )
+
+
 def solution(mesh):
     in_specs = (
         P(None, "ctx", None),

time: 469 us -> 67 us (0.14)
  waiting for transfers between devices: 160 us -> 0 us
  blocking collectives: 92.9 us -> 0 us
  local copies, waits for them, and re-layouts: 85.4 us -> 0.67 us
  other arithmetic: 62.6 us -> 0 us
  Pallas kernels: 0 us -> 51.9 us
  matrix products: 26 us -> 0 us
  starting transfers between devices: 23.2 us -> 0 us
    all_to_all x3 -> x0, waiting for transfers between devices: 160 us -> none  [move_suffix(): lax.all_to_all(outbound, 'br', split_axis=0, concat_axis=0, tiled=True)]
    all_gather x7 -> x0, blocking collectives: 92.9 us -> none  [the longest x6 79 us: joined_2(): gathered = jax.tree.map(lambda a: lax.all_gather(a, axis), part)]
    pallas_call x0 -> x1, Pallas kernels: none -> 51.9 us  [local(): pl.pallas_call(functools.partial(kernel, br_count, ctx_count), out_shape=...]
    add x46 -> x0, other arithmetic: 37.9 us -> none  [the longest x21 30.4 us: fold_pair(): left_stats[2] * left_weight[..., None]]
    gather x10 -> x0, local copies, waits for them, and re-layouts: 33.8 us -> none  [the longest x3 12 us: move_suffix(): return arrived.reshape((dest_count * slot_count,) + tail_shape)[incoming]]
    unnamed x107 -> x13, local copies, waits for them, and re-layouts: 28.1 us -> 0.67 us
    dot_general x12 -> x0, matrix products: 26 us -> none  [the longest x6 12.5 us: block_stats(): jnp.einsum(einsum_form, rounded, values, preferred_element_type=jnp.float32)]
    all_to_all x3 -> x0, starting transfers between devices: 22.9 us -> none  [move_suffix(): lax.all_to_all(outbound, 'br', split_axis=0, concat_axis=0, tiled=True)]
  transfers between devices with their start and end apart: 6 -> 0, of which waited for: 3 -> 0; matrix products, arithmetic and copies ran while one was open for 29% -> 0% of each run, Pallas kernels for 0% -> 0%
where the time goes in v3:
time: 67 us; the launch traced here: 66.9 us
  Pallas kernels  51.9 us (77%)
  between operations  14.1 us (21%)
  local copies, waits for them, and re-layouts  0.67 us (1%)
    pallas_call x1, Pallas kernels, local(): pl.pallas_call(functools.partial(kernel, br_count, ctx_count), out_shape=...  51.9 us

profile of v3, /device:TPU:6, one launch (start us, length us, event | category | flops | bytes accessed | tf_op | source)
XLA Modules:
  0.0 66.9 jit_solution(2299338172817527423)
XLA Ops:
  6.5 0.0 copy-start
  6.5 0.0 copy-start.7
  6.5 0.0 copy-start.10
  6.5 0.0 copy-start.27
  6.5 0.0 copy-start.28
  6.5 0.0 copy-start.36
  6.6 51.9 %shard_map.75 = (bf16[48,1024]{1,0:T(8,128)(2,1)S(1)}, s32[1,1]{1,0:T(1,128)}) custom-call(s32[2,16]{1,0:T(2,128)} %bitcast.447, s32[512]{0:T(512)} %len_ref.1, s32[3,512]{1,0:T(4,128)} %par_ref.1, bf16[48,1024]{1,0:T(8,128)(2,1)} %bitcast.430, bf16[3,2,16,128]{3,2,1,0:T(8,128)(2,1)} %fresh_ref.1, bf16[2,2048,1024]{2,1,0:T(8,128)(2,1)} %pkv_ref.1, ...), custom_call_target="tpu_custom_call" | custom-call | tf_op jit(solution)/shard_map/pallas_call | solution.py:721
  59.1 0.0 copy-done
  59.1 0.0 copy-done.7
  59.1 0.0 copy-done.10
  59.1 0.0 copy-done.27
  59.1 0.0 copy-done.28
  59.1 0.0 copy-done.36
  59.1 0.3 conditional.1
  59.4 0.6 copy.301
Async XLA Ops:
  6.5 52.5 %copy-start = (s32[512]{0:T(512)S(1)}, s32[512]{0:T(512)}, u32[]{:S(2)}) copy-start(s32[512]{0:T(512)} %len_ref.1) | copy-start | bytes 6148
  6.5 52.5 %copy-start.7 = (bf16[32,2,128,128]{3,2,1,0:T(8,128)(2,1)S(1)}, bf16[32,2,128,128]{3,2,1,0:T(8,128)(2,1)}, u32[]{:S(2)}) copy-start(bf16[32,2,128,128]{3,2,1,0:T(8,128)(2,1)} %pages_ref.1) | copy-start | bytes 6291460
  6.5 52.5 %copy-start.10 = (bf16[3,16,1024]{2,1,0:T(8,128)(2,1)S(1)}, bf16[3,16,1024]{2,1,0:T(8,128)(2,1)}, u32[]{:S(2)}) copy-start(bf16[3,16,1024]{2,1,0:T(8,128)(2,1)} %param.20) | copy-start | bytes 294916
  6.5 52.6 %copy-start.27 = (bf16[3,2,16,128]{3,2,1,0:T(8,128)(2,1)S(1)}, bf16[3,2,16,128]{3,2,1,0:T(8,128)(2,1)}, u32[]{:S(2)}) copy-start(bf16[3,2,16,128]{3,2,1,0:T(8,128)(2,1)} %fresh_ref.1) | copy-start | bytes 73732
  6.5 52.6 %copy-start.28 = (s32[3,512]{1,0:T(4,128)S(1)}, s32[3,512]{1,0:T(4,128)}, u32[]{:S(2)}) copy-start(s32[3,512]{1,0:T(4,128)} %par_ref.1) | copy-start | bytes 18436
  6.5 52.6 %copy-start.36 = (s32[16,2]{0,1:T(2,128)S(1)}, s32[16,2]{0,1:T(2,128)}, u32[]{:S(2)}) copy-start(s32[16,2]{0,1:T(2,128)} %param.17) | copy-start | bytes 388

commit v4 on v3

--- a/solution.py
+++ b/solution.py
@@ -488,14 +488,17 @@
                 stat = jnp.where(stat_lane == 8 + h, total[cut], stat)
         part_send[where, pl.ds(ROWS, NODES)] = stat
 
-    prompt_block(0, 0)
-
-    @pl.loop(1, chips)
-    def _(t):
+    def prompt_head(t):
         query_copy(t, chip_at(t)).wait_recv()
         prompt_block(t, 0)
         prompt_block(t, 1)
         part_copy(t, chip).start()
+
+    prompt_block(0, 0)
+
+    @pl.loop(1, chips - 1)
+    def _(t):
+        prompt_head(t)
 
     @pl.loop(1, br_count)
     def _(i):
@@ -606,8 +609,6 @@
     give_back(0, stat_rows(stat_a, slice(0, LIVE)),
               return_rows(quad_row[:, :LIVE], code_high[...], code_low[...]))
 
-    prompt_block(0, 1)
-
     @pl.loop(1, br_count)
     def _(i):
         message_b(0, peer_r(i)).wait_recv()
@@ -628,6 +629,9 @@
         stat_b = jnp.where(late_lane == 8 + h, unit[cut], stat_b)
     give_back(1, stat_rows(stat_b, late),
               return_rows(quad_row[:, late] - QUAD, late_high[...], late_low[...]))
+
+    prompt_head(chips - 1)
+    prompt_block(0, 1)
 
     part_recv[chip] = part_send[chip]
 

time: 67 us -> 64.4 us (0.961)
  Pallas kernels: 51.9 us -> 49.3 us
    pallas_call x1, Pallas kernels: 51.9 us -> 49.3 us  [local(): pl.pallas_call(functools.partial(kernel, br_count, ctx_count), out_shape=...]
where the time goes in v4:
time: 64.4 us; the launch traced here: 64.3 us
  Pallas kernels  49.3 us (77%)
  between operations  14.1 us (22%)
  local copies, waits for them, and re-layouts  0.67 us (1%)
    pallas_call x1, Pallas kernels, local(): pl.pallas_call(functools.partial(kernel, br_count, ctx_count), out_shape=...  49.3 us

profile of v4, /device:TPU:6, one launch (start us, length us, event | category | flops | bytes accessed | tf_op | source)
XLA Modules:
  0.0 64.3 jit_solution(7713236557292751533)
XLA Ops:
  6.5 0.0 copy-start
  6.5 0.0 copy-start.7
  6.5 0.0 copy-start.10
  6.5 0.0 copy-start.27
  6.5 0.0 copy-start.28
  6.5 0.0 copy-start.36
  6.6 49.3 %shard_map.75 = (bf16[48,1024]{1,0:T(8,128)(2,1)S(1)}, s32[1,1]{1,0:T(1,128)}) custom-call(s32[2,16]{1,0:T(2,128)} %bitcast.447, s32[512]{0:T(512)} %len_ref.1, s32[3,512]{1,0:T(4,128)} %par_ref.1, bf16[48,1024]{1,0:T(8,128)(2,1)} %bitcast.430, bf16[3,2,16,128]{3,2,1,0:T(8,128)(2,1)} %fresh_ref.1, bf16[2,2048,1024]{2,1,0:T(8,128)(2,1)} %pkv_ref.1, ...), custom_call_target="tpu_custom_call" | custom-call | tf_op jit(solution)/shard_map/pallas_call | solution.py:725
  56.5 0.0 copy-done
  56.5 0.0 copy-done.7
  56.5 0.0 copy-done.10
  56.5 0.0 copy-done.27
  56.5 0.0 copy-done.28
  56.6 0.0 copy-done.36
  56.6 0.3 conditional.1
  56.8 0.6 copy.301
Async XLA Ops:
  6.5 50.0 %copy-start = (s32[512]{0:T(512)S(1)}, s32[512]{0:T(512)}, u32[]{:S(2)}) copy-start(s32[512]{0:T(512)} %len_ref.1) | copy-start | bytes 6148
  6.5 50.0 %copy-start.7 = (bf16[32,2,128,128]{3,2,1,0:T(8,128)(2,1)S(1)}, bf16[32,2,128,128]{3,2,1,0:T(8,128)(2,1)}, u32[]{:S(2)}) copy-start(bf16[32,2,128,128]{3,2,1,0:T(8,128)(2,1)} %pages_ref.1) | copy-start | bytes 6291460
  6.5 50.0 %copy-start.10 = (bf16[3,16,1024]{2,1,0:T(8,128)(2,1)S(1)}, bf16[3,16,1024]{2,1,0:T(8,128)(2,1)}, u32[]{:S(2)}) copy-start(bf16[3,16,1024]{2,1,0:T(8,128)(2,1)} %param.20) | copy-start | bytes 294916
  6.5 50.0 %copy-start.27 = (bf16[3,2,16,128]{3,2,1,0:T(8,128)(2,1)S(1)}, bf16[3,2,16,128]{3,2,1,0:T(8,128)(2,1)}, u32[]{:S(2)}) copy-start(bf16[3,2,16,128]{3,2,1,0:T(8,128)(2,1)} %fresh_ref.1) | copy-start | bytes 73732
  6.5 50.0 %copy-start.28 = (s32[3,512]{1,0:T(4,128)S(1)}, s32[3,512]{1,0:T(4,128)}, u32[]{:S(2)}) copy-start(s32[3,512]{1,0:T(4,128)} %par_ref.1) | copy-start | bytes 18436
  6.5 50.0 %copy-start.36 = (s32[16,2]{0,1:T(2,128)S(1)}, s32[16,2]{0,1:T(2,128)}, u32[]{:S(2)}) copy-start(s32[16,2]{0,1:T(2,128)} %param.17) | copy-start | bytes 388

commit v5 on v4

--- a/solution.py
+++ b/solution.py
@@ -385,15 +385,18 @@
     @pl.loop(1, chips)
     def _(t):
         query_copy(t, chip).start()
-        kv_give(t, 0).start()
-        kv_give(t, 1).start()
-
-    kv_give(0, 0).start()
-    kv_give(0, 1).start()
 
     @pl.loop(1, br_count)
     def _(i):
         message_a(i, me_r).start()
+
+    @pl.loop(1, chips)
+    def _(t):
+        kv_give(t, 0).start()
+        kv_give(t, 1).start()
+
+    kv_give(0, 0).start()
+    kv_give(0, 1).start()
 
     @pl.loop(1, br_count)
     def _(i):

time: 64.4 us -> 64.4 us (level)
  no operation moved by 1% of the time
where the time goes in v5:
time: 64.4 us; the launch traced here: 64.3 us
  Pallas kernels  49.3 us (77%)
  between operations  14.1 us (22%)
  local copies, waits for them, and re-layouts  0.67 us (1%)
    pallas_call x1, Pallas kernels, local(): pl.pallas_call(functools.partial(kernel, br_count, ctx_count), out_shape=...  49.3 us

profile of v5, /device:TPU:6, one launch (start us, length us, event | category | flops | bytes accessed | tf_op | source)
XLA Modules:
  0.0 64.3 jit_solution(16295850417572080176)
XLA Ops:
  6.5 0.0 copy-start
  6.5 0.0 copy-start.7
  6.5 0.0 copy-start.10
  6.5 0.0 copy-start.27
  6.5 0.0 copy-start.28
  6.5 0.0 copy-start.36
  6.6 49.3 %shard_map.75 = (bf16[48,1024]{1,0:T(8,128)(2,1)S(1)}, s32[1,1]{1,0:T(1,128)}) custom-call(s32[2,16]{1,0:T(2,128)} %bitcast.447, s32[512]{0:T(512)} %len_ref.1, s32[3,512]{1,0:T(4,128)} %par_ref.1, bf16[48,1024]{1,0:T(8,128)(2,1)} %bitcast.430, bf16[3,2,16,128]{3,2,1,0:T(8,128)(2,1)} %fresh_ref.1, bf16[2,2048,1024]{2,1,0:T(8,128)(2,1)} %pkv_ref.1, ...), custom_call_target="tpu_custom_call" | custom-call | tf_op jit(solution)/shard_map/pallas_call | solution.py:728
  56.5 0.0 copy-done
  56.5 0.0 copy-done.7
  56.6 0.0 copy-done.10
  56.6 0.0 copy-done.27
  56.6 0.0 copy-done.28
  56.6 0.0 copy-done.36
  56.6 0.3 conditional.1
  56.9 0.6 copy.301
Async XLA Ops:
  6.5 50.0 %copy-start = (s32[512]{0:T(512)S(1)}, s32[512]{0:T(512)}, u32[]{:S(2)}) copy-start(s32[512]{0:T(512)} %len_ref.1) | copy-start | bytes 6148
  6.5 50.0 %copy-start.7 = (bf16[32,2,128,128]{3,2,1,0:T(8,128)(2,1)S(1)}, bf16[32,2,128,128]{3,2,1,0:T(8,128)(2,1)}, u32[]{:S(2)}) copy-start(bf16[32,2,128,128]{3,2,1,0:T(8,128)(2,1)} %pages_ref.1) | copy-start | bytes 6291460
  6.5 50.0 %copy-start.10 = (bf16[3,16,1024]{2,1,0:T(8,128)(2,1)S(1)}, bf16[3,16,1024]{2,1,0:T(8,128)(2,1)}, u32[]{:S(2)}) copy-start(bf16[3,16,1024]{2,1,0:T(8,128)(2,1)} %param.20) | copy-start | bytes 294916
  6.5 50.0 %copy-start.27 = (bf16[3,2,16,128]{3,2,1,0:T(8,128)(2,1)S(1)}, bf16[3,2,16,128]{3,2,1,0:T(8,128)(2,1)}, u32[]{:S(2)}) copy-start(bf16[3,2,16,128]{3,2,1,0:T(8,128)(2,1)} %fresh_ref.1) | copy-start | bytes 73732
  6.5 50.0 %copy-start.28 = (s32[3,512]{1,0:T(4,128)S(1)}, s32[3,512]{1,0:T(4,128)}, u32[]{:S(2)}) copy-start(s32[3,512]{1,0:T(4,128)} %par_ref.1) | copy-start | bytes 18436
  6.5 50.0 %copy-start.36 = (s32[16,2]{0,1:T(2,128)S(1)}, s32[16,2]{0,1:T(2,128)}, u32[]{:S(2)}) copy-start(s32[16,2]{0,1:T(2,128)} %param.17) | copy-start | bytes 388

commit v6 on v5

--- a/solution.py
+++ b/solution.py
@@ -229,7 +229,7 @@
     page_ref, len_ref, par_ref, q_ref, fresh_ref, pkv_ref, pages_ref,
     out_ref, flag_ref,
     kbuf, vbuf, kpage, vpage, qbuf, send_a, recv_a, send_b, recv_b, qrows, part_send, part_recv,
-    code_high, code_low, late_high, late_low, stat_send, stat_recv, ret_send, ret_recv, num,
+    code_high, code_low, late_high, late_low, stat_send, stat_recv, ret_send, ret_recv, late_send, late_recv, num,
     kv_sem, g_send, g_recv, page_sem, q_send, q_recv, a_send, a_recv, b_send, b_recv, p_send, p_recv,
     r_send, r_recv, s_send, s_recv,
 ):
@@ -522,8 +522,9 @@
 
     taken = gathered(quad_col[:LIVE], got_a[:, :256])
     for n in range(4):
-        for half in range(2):
-            qrows[n, pl.ds(half * LIVE, LIVE)] = taken[n * LIVE:(n + 1) * LIVE, half * 128:(half + 1) * 128]
+        for parity in range(2):
+            qrows[2 * parity + n // 2, pl.ds((n % 2) * LIVE, LIVE)] = taken[
+                n * LIVE:(n + 1) * LIVE, parity * 128:(parity + 1) * 128]
     key_pages.wait()
     value_pages.wait()
 
@@ -571,7 +572,9 @@
         return (256.0 * dot(spread, high) + dot(spread, low)).astype(jnp.int32).astype(jnp.int16)
 
     def returned(group, i, source):
-        return to_br(i, source, ret_send.at[group], ret_recv.at[group], r_send.at[group], r_recv.at[group])
+        if group < 2:
+            return to_br(i, source, ret_send.at[group], ret_recv.at[group], r_send.at[group], r_recv.at[group])
+        return to_br(i, source, late_send, late_recv, r_send.at[2], r_recv.at[2])
 
     def returned_stat(group, i, source):
         peer = peer_r(i)
@@ -580,37 +583,44 @@
             send_sem=s_send.at[group, peer], recv_sem=s_recv.at[group, source],
             device_id={"br": peer}, device_id_type=pl.DeviceIdType.MESH)
 
-    def give_back(group, stat, rows):
+    def give_stat(group, stat):
         for home_index in range(br_count):
             stat_send[group, home_index] = stat[home_index:home_index + 1]
-        ret_send[group] = rows
 
         @pl.loop(1, br_count)
         def _(i):
             returned_stat(group, i, me_r).start()
-            returned(group, i, me_r).start()
 
         stat_recv[group, me_r] = stat_send[group, me_r]
-        ret_recv[group, own16, :] = ret_send[group, own16, :]
 
     first_lane = iota((LIVE, 128), 1) & 15
-
-    def suffix_quarter(n, stat):
-        high, low, sum_log, unit = suffix_block(
-            qrows[n], repeated(anc_col[:LIVE], 2), repeated(length_col[:LIVE], 2), repeated(path[:LIVE], 2))
-        quarter = pl.ds(pl.multiple_of(n * LIVE, LIVE), LIVE)
-        for half in range(2):
-            cut = slice(half * LIVE, (half + 1) * LIVE)
-            code_high[quarter, pl.ds(half * 128, 128)] = high[cut]
-            code_low[quarter, pl.ds(half * 128, 128)] = low[cut]
-            stat = jnp.where(first_lane == 2 * n + half, sum_log[cut], stat)
-            stat = jnp.where(first_lane == 8 + 2 * n + half, unit[cut], stat)
-        return stat
-
-    stat_a = lax.fori_loop(0, 4, suffix_quarter, jnp.zeros((LIVE, 128), F32))
-
-    give_back(0, stat_rows(stat_a, slice(0, LIVE)),
-              return_rows(quad_row[:, :LIVE], code_high[...], code_low[...]))
+    stat_a = jnp.zeros((LIVE, 128), F32)
+    for parity in range(2):
+
+        def suffix_pair(pair, stat):
+            high, low, sum_log, unit = suffix_block(
+                qrows[2 * parity + pair], repeated(anc_col[:LIVE], 2), repeated(length_col[:LIVE], 2),
+                repeated(path[:LIVE], 2))
+            pair_rows = pl.ds(pl.multiple_of(pair * 2 * LIVE, 2 * LIVE), 2 * LIVE)
+            code_high[pair_rows] = high
+            code_low[pair_rows] = low
+            for half in range(2):
+                cut = slice(half * LIVE, (half + 1) * LIVE)
+                head = 4 * pair + 2 * half + parity
+                stat = jnp.where(first_lane == head, sum_log[cut], stat)
+                stat = jnp.where(first_lane == 8 + head, unit[cut], stat)
+            return stat
+
+        stat_a = lax.fori_loop(0, 2, suffix_pair, stat_a)
+        ret_send[parity] = return_rows(quad_row[:, :LIVE], code_high[...], code_low[...])
+
+        @pl.loop(1, br_count)
+        def _(i):
+            returned(parity, i, me_r).start()
+
+        ret_recv[parity, own16, :] = ret_send[parity, own16, :]
+
+    give_stat(0, stat_rows(stat_a, slice(0, LIVE)))
 
     @pl.loop(1, br_count)
     def _(i):
@@ -630,8 +640,14 @@
         late_low[pl.ds((h // 2) * LATE, LATE), pl.ds((h % 2) * 128, 128)] = low[cut]
         stat_b = jnp.where(late_lane == h, sum_log[cut], stat_b)
         stat_b = jnp.where(late_lane == 8 + h, unit[cut], stat_b)
-    give_back(1, stat_rows(stat_b, late),
-              return_rows(quad_row[:, late] - QUAD, late_high[...], late_low[...]))
+    late_send[...] = return_rows(quad_row[:, late] - QUAD, late_high[...], late_low[...])
+
+    @pl.loop(1, br_count)
+    def _(i):
+        returned(2, i, me_r).start()
+
+    late_recv[own16, :] = late_send[own16, :]
+    give_stat(1, stat_rows(stat_b, late))
 
     prompt_head(chips - 1)
     prompt_block(0, 1)
@@ -658,28 +674,32 @@
     address = repeated(own_dev * QUAD + own_slot, 4)
     quarter_at = iota((4 * NODES, 16 * br_count), 0) // NODES
 
-    def collected(group, match):
+    def collected(arrived, match):
         collect = onehot(match & ((back_low & 3) == quarter_at))
-        arrived = ret_recv[group].astype(jnp.int32)
+        arrived = arrived.astype(jnp.int32)
         upper = dot(collect, (arrived >> 8).astype(F32).astype(BF))
         return 256.0 * upper + dot(collect, (arrived & 255).astype(F32).astype(BF))
 
     in_first = repeated(own_slot, 4) < QUAD
     quad_at = (back_low >> 2).astype(F32)
+    first_match = in_first & (quad_at == address)
+    coded = []
+    for parity in range(2):
+
+        @pl.loop(1, br_count)
+        def _(i):
+            returned(parity, 0, peer_r(i)).wait_recv()
+
+        coded.append(collected(ret_recv[parity], first_match))
 
     @pl.loop(1, br_count)
     def _(i):
+        returned(2, 0, peer_r(i)).wait_recv()
         returned_stat(0, 0, peer_r(i)).wait_recv()
-        returned(0, 0, peer_r(i)).wait_recv()
-
-    coded = collected(0, in_first & (quad_at == address))
-
-    @pl.loop(1, br_count)
-    def _(i):
         returned_stat(1, 0, peer_r(i)).wait_recv()
-        returned(1, 0, peer_r(i)).wait_recv()
-
-    coded = coded + collected(1, jnp.logical_not(in_first) & (quad_at == address - QUAD))
+
+    coded_late = collected(late_recv[...], jnp.logical_not(in_first) & (quad_at == address - QUAD))
+    coded = jnp.concatenate(coded, axis=1) + coded_late
     from_device = jnp.where(iota((NODES, br_count), 1).astype(F32) == own_dev, 1.0, 0.0)
     all_stat = jnp.concatenate([stat_recv[0, d] + stat_recv[1, d] for d in range(br_count)], axis=0)
     back_stat = jnp.dot(from_device, all_stat, precision=lax.Precision.HIGHEST, preferred_element_type=F32)
@@ -713,6 +733,7 @@
         message_b(i, me_r).wait_send()
         for group in range(2):
             returned_stat(group, i, me_r).wait_send()
+        for group in range(3):
             returned(group, i, me_r).wait_send()
 
 
@@ -746,17 +767,19 @@
             pltpu.VMEM((4, 2 * LIVE, 128), BF),
             pltpu.VMEM((4, ROWS + NODES, 128), F32),
             pltpu.VMEM((4, ROWS + NODES, 128), F32),
-            pltpu.VMEM((4 * LIVE, 256), BF),
-            pltpu.VMEM((4 * LIVE, 256), BF),
+            pltpu.VMEM((4 * LIVE, 128), BF),
+            pltpu.VMEM((4 * LIVE, 128), BF),
             pltpu.VMEM((4 * LATE, 256), BF),
             pltpu.VMEM((4 * LATE, 256), BF),
             pltpu.VMEM((2, br_count, 1, 128), F32),
             pltpu.VMEM((2, br_count, 1, 128), F32),
-            pltpu.VMEM((2, 16 * br_count, 256), jnp.int16),
-            pltpu.VMEM((2, 16 * br_count, 256), jnp.int16),
+            pltpu.VMEM((2, 16 * br_count, 128), jnp.int16),
+            pltpu.VMEM((2, 16 * br_count, 128), jnp.int16),
+            pltpu.VMEM((16 * br_count, 256), jnp.int16),
+            pltpu.VMEM((16 * br_count, 256), jnp.int16),
             pltpu.VMEM((8, NODES, 128), F32),
             dma((2, 4)), dma((2, 4)), dma((2, 4)), dma((2,)), dma((4,)), dma((4,)), dma((32,)), dma((32,)), dma((32,)), dma((32,)),
-            dma((4,)), dma((4,)), dma((2, 32)), dma((2, 32)), dma((2, 32)), dma((2, 32)),
+            dma((4,)), dma((4,)), dma((3, 32)), dma((3, 32)), dma((2, 32)), dma((2, 32)),
         ],
         compiler_params=pltpu.CompilerParams(
             collective_id=0, has_side_effects=True, vmem_limit_bytes=56 * 1024 * 1024

time: 64.4 us -> 67.1 us (1.042)
  the two profiles are of different devices: /device:TPU:6 before, /device:TPU:8 now
where the time goes in v6:
time: 67.1 us; the launch traced here: 67 us
  Pallas kernels  52 us (77%)
  between operations  14.1 us (21%)
    pallas_call x1, Pallas kernels, local(): pl.pallas_call(functools.partial(kernel, br_count, ctx_count), out_shape=...  52 us

profile of v6, /device:TPU:8, one launch (start us, length us, event | category | flops | bytes accessed | tf_op | source)
XLA Modules:
  0.0 67.0 jit_solution(8061370686728459321)
XLA Ops:
  6.5 0.0 copy-start
  6.5 0.0 copy-start.7
  6.5 0.0 copy-start.10
  6.5 0.0 copy-start.27
  6.5 0.0 copy-start.28
  6.5 0.0 copy-start.36
  6.6 52.0 %shard_map.75 = (bf16[48,1024]{1,0:T(8,128)(2,1)S(1)}, s32[1,1]{1,0:T(1,128)}) custom-call(s32[2,16]{1,0:T(2,128)} %bitcast.447, s32[512]{0:T(512)} %len_ref.1, s32[3,512]{1,0:T(4,128)} %par_ref.1, bf16[48,1024]{1,0:T(8,128)(2,1)} %bitcast.430, bf16[3,2,16,128]{3,2,1,0:T(8,128)(2,1)} %fresh_ref.1, bf16[2,2048,1024]{2,1,0:T(8,128)(2,1)} %pkv_ref.1, ...), custom_call_target="tpu_custom_call" | custom-call | tf_op jit(solution)/shard_map/pallas_call | solution.py:749
  59.2 0.0 copy-done
  59.2 0.0 copy-done.7
  59.2 0.0 copy-done.10
  59.2 0.0 copy-done.27
  59.3 0.0 copy-done.28
  59.3 0.0 copy-done.36
  59.3 0.3 conditional.1
  59.5 0.6 copy.301
Async XLA Ops:
  6.5 52.7 %copy-start = (s32[512]{0:T(512)S(1)}, s32[512]{0:T(512)}, u32[]{:S(2)}) copy-start(s32[512]{0:T(512)} %len_ref.1) | copy-start | bytes 6148
  6.5 52.7 %copy-start.7 = (bf16[32,2,128,128]{3,2,1,0:T(8,128)(2,1)S(1)}, bf16[32,2,128,128]{3,2,1,0:T(8,128)(2,1)}, u32[]{:S(2)}) copy-start(bf16[32,2,128,128]{3,2,1,0:T(8,128)(2,1)} %pages_ref.1) | copy-start | bytes 6291460
  6.5 52.7 %copy-start.10 = (bf16[3,16,1024]{2,1,0:T(8,128)(2,1)S(1)}, bf16[3,16,1024]{2,1,0:T(8,128)(2,1)}, u32[]{:S(2)}) copy-start(bf16[3,16,1024]{2,1,0:T(8,128)(2,1)} %param.20) | copy-start | bytes 294916
  6.5 52.7 %copy-start.27 = (bf16[3,2,16,128]{3,2,1,0:T(8,128)(2,1)S(1)}, bf16[3,2,16,128]{3,2,1,0:T(8,128)(2,1)}, u32[]{:S(2)}) copy-start(bf16[3,2,16,128]{3,2,1,0:T(8,128)(2,1)} %fresh_ref.1) | copy-start | bytes 73732
  6.5 52.7 %copy-start.28 = (s32[3,512]{1,0:T(4,128)S(1)}, s32[3,512]{1,0:T(4,128)}, u32[]{:S(2)}) copy-start(s32[3,512]{1,0:T(4,128)} %par_ref.1) | copy-start | bytes 18436
  6.5 52.7 %copy-start.36 = (s32[16,2]{0,1:T(2,128)S(1)}, s32[16,2]{0,1:T(2,128)}, u32[]{:S(2)}) copy-start(s32[16,2]{0,1:T(2,128)} %param.17) | copy-start | bytes 388
